TPU v7x, 32 devices: a whole 2x2x4 slice. The times are simulated.
32 devices in a mesh: replica: 8 (over y, x, core), fsdp: 4 (over z).
Axes of the slice: x: 2, y: 2, z: 4, core: 2. Of those that a mesh axis runs over, the one named last changes fastest.
Arguments:
- tokens: bfloat16 [12288, 2048], P(('replica', 'fsdp')), may hold values from -24 to 24
- cotangent: bfloat16 [12288, 2048], P(('replica', 'fsdp')), may hold values from -6 to 6
- w_query: bfloat16 [8, 2048, 2048], P('replica', 'fsdp'), may hold values from -0.125 to 0.125
- replica_key_weight: bfloat16 [8, 2048, 512], P('replica', 'fsdp'), may hold values from -0.125 to 0.125
- replica_value_weight: bfloat16 [8, 2048, 512], P('replica', 'fsdp'), may hold values from -0.125 to 0.125
- w_output: bfloat16 [8, 2048, 2048], P('replica', None, 'fsdp'), may hold values from -0.125 to 0.125
- snapshot: bfloat16 [8, 2048, 2048], P('replica', None, 'fsdp'), may hold values from -0.1875 to 0.1875
- global_output: float32 [2048, 2048], P('replica', 'fsdp'), may hold values from -0.125 to 0.125
- momentum: float32 [2048, 2048], P('replica', 'fsdp'), may hold values from -0.18 to 0.18
Outputs:
- block_out: bfloat16 [12288, 2048], P(('replica', 'fsdp'))
- grad_query: bfloat16 [8, 2048, 2048], P('replica', 'fsdp')
- grad_key: bfloat16 [8, 2048, 512], P('replica', 'fsdp')
- grad_value: bfloat16 [8, 2048, 512], P('replica', 'fsdp')
- grad_output: bfloat16 [8, 2048, 2048], P('replica', None, 'fsdp')
- merged_output: bfloat16 [8, 2048, 2048], P('replica', None, 'fsdp')
- global_new: float32 [2048, 2048], P('replica', 'fsdp')
- momentum_new: float32 [2048, 2048], P('replica', 'fsdp')
All inputs are finite; a program needn't handle non-finite values.
Results may differ from a plain program's by a relative error of at most 0.015.
The roundings to bfloat16 on the way count: a program that leaves them out, or rounds other values in their place, can miss the bound.
Values may be sent and summed in bfloat16 or wider, within the bound.
A program may use at most 192 MiB of HBM per device.

v0:
```python
import jax
import jax.numpy as jnp
from jax import lax
from jax.sharding import PartitionSpec as P

HEAD_SIZE = 128
QUERY_HEADS = 16
KEYVALUE_HEADS = 4


theta_base = 500000.0
momentum_decay = 0.9
outer_rate = 0.7
mixing = 0.5


def apply_rotation(value_rows, sign):
    sequence_length = value_rows.shape[0]
    half = value_rows.shape[2] // 2
    position = jnp.arange(sequence_length).astype(jnp.float32)
    freq = jnp.exp(
        -jnp.log(theta_base) * jnp.arange(half).astype(jnp.float32) * 2.0 / value_rows.shape[2]
    )
    angle = position[:, None] * freq[None, :]
    cosine = jnp.cos(angle)[:, None, :]
    sine = sign * jnp.sin(angle)[:, None, :]
    first = value_rows[..., :half]
    second = value_rows[..., half:]
    return jnp.concatenate(
        [first * cosine - second * sine, first * sine + second * cosine], axis=-1
    )


def attend_forward(query_unrotated, key_unrotated, value_unprojected):
    sequence_length = query_unrotated.shape[0]
    head_group = QUERY_HEADS // KEYVALUE_HEADS
    scale = HEAD_SIZE ** (-0.5)
    query_rows = (
        apply_rotation(query_unrotated.reshape(sequence_length, QUERY_HEADS, HEAD_SIZE), 1.0)
        .astype(jnp.bfloat16)
        .reshape(sequence_length, KEYVALUE_HEADS, head_group, HEAD_SIZE)
    )
    key_rows = apply_rotation(
        key_unrotated.reshape(sequence_length, KEYVALUE_HEADS, HEAD_SIZE), 1.0
    ).astype(jnp.bfloat16)
    value_rows = value_unprojected.astype(jnp.bfloat16).reshape(
        sequence_length, KEYVALUE_HEADS, HEAD_SIZE
    )
    scores = (
        jnp.einsum("qkgd,skd->kgqs", query_rows, key_rows, preferred_element_type=jnp.float32)
        * scale
    )
    causal = jnp.arange(sequence_length)[:, None] >= jnp.arange(sequence_length)[None, :]
    scores = jnp.where(causal, scores, -1e30)
    top = jnp.max(scores, axis=-1, keepdims=True)
    expo = jnp.exp(scores - top)
    probs = expo / jnp.sum(expo, axis=-1, keepdims=True)
    probs_b = probs.astype(jnp.bfloat16)
    attn = jnp.einsum("kgqs,skd->qkgd", probs_b, value_rows, preferred_element_type=jnp.float32)
    attn = attn.astype(jnp.bfloat16).reshape(sequence_length, QUERY_HEADS * HEAD_SIZE)
    return (attn, (query_rows, key_rows, value_rows, probs, probs_b))


def attend_backward(saved, attention_gradient):
    query_rows, key_rows, value_rows, probs, probs_b = saved
    sequence_length = query_rows.shape[0]
    head_group = QUERY_HEADS // KEYVALUE_HEADS
    scale = HEAD_SIZE ** (-0.5)
    output_gradient = attention_gradient.reshape(
        sequence_length, KEYVALUE_HEADS, head_group, HEAD_SIZE
    )
    value_gradient = jnp.einsum(
        "kgqs,qkgd->skd", probs_b, output_gradient, preferred_element_type=jnp.float32
    )
    d_probs = jnp.einsum(
        "qkgd,skd->kgqs", output_gradient, value_rows, preferred_element_type=jnp.float32
    )
    d_scores = (probs * (d_probs - jnp.sum(d_probs * probs, axis=-1, keepdims=True))).astype(
        jnp.bfloat16
    )
    query_gradient = (
        jnp.einsum("kgqs,skd->qkgd", d_scores, key_rows, preferred_element_type=jnp.float32) * scale
    )
    key_gradient = (
        jnp.einsum("kgqs,qkgd->skd", d_scores, query_rows, preferred_element_type=jnp.float32)
        * scale
    )
    query_gradient = apply_rotation(
        query_gradient.reshape(sequence_length, QUERY_HEADS, HEAD_SIZE), -1.0
    ).reshape(sequence_length, QUERY_HEADS * HEAD_SIZE)
    key_gradient = apply_rotation(key_gradient, -1.0).reshape(
        sequence_length, KEYVALUE_HEADS * HEAD_SIZE
    )
    projection_gradient = jnp.concatenate(
        [
            query_gradient,
            key_gradient,
            value_gradient.reshape(sequence_length, KEYVALUE_HEADS * HEAD_SIZE),
        ],
        axis=1,
    )
    return projection_gradient.astype(jnp.bfloat16)


def outer_sync(snapshot, global_output, momentum, w_output):
    total = lax.psum_scatter(
        snapshot[0].astype(jnp.float32), "replica", scatter_dimension=0, tiled=True
    )
    mean_snapshot = total / lax.axis_size("replica")
    delta = global_output - mean_snapshot
    momentum_new = momentum_decay * momentum + delta
    global_new = global_output - outer_rate * (delta + momentum_decay * momentum_new)
    gathered = lax.all_gather(global_new, "replica", axis=0, tiled=True)
    merged = (mixing * w_output[0].astype(jnp.float32) + (1.0 - mixing) * gathered).astype(
        jnp.bfloat16
    )
    return (merged[None], global_new, momentum_new)


def per_device(
    tokens,
    cotangent,
    w_query,
    replica_key_weight,
    replica_value_weight,
    w_output,
    snapshot,
    global_output,
    momentum,
):
    query_cols = w_query.shape[2]
    key_cols = replica_key_weight.shape[2]
    columns = tokens
    query_unrotated = jnp.dot(
        columns,
        lax.all_gather(w_query[0], "fsdp", axis=0, tiled=True),
        preferred_element_type=jnp.float32,
    )
    key_unrotated = jnp.dot(
        columns,
        lax.all_gather(replica_key_weight[0], "fsdp", axis=0, tiled=True),
        preferred_element_type=jnp.float32,
    )
    value_unprojected = jnp.dot(
        columns,
        lax.all_gather(replica_value_weight[0], "fsdp", axis=0, tiled=True),
        preferred_element_type=jnp.float32,
    )
    attn, saved = attend_forward(query_unrotated, key_unrotated, value_unprojected)
    whole_output = lax.all_gather(w_output[0], "fsdp", axis=1, tiled=True)
    block_out = (
        tokens.astype(jnp.float32) + jnp.dot(attn, whole_output, preferred_element_type=jnp.float32)
    ).astype(jnp.bfloat16)
    attention_gradient = lax.dot_general(
        cotangent, whole_output, (((1,), (1,)), ((), ())), preferred_element_type=jnp.float32
    ).astype(jnp.bfloat16)
    term_output = lax.dot_general(
        attn, cotangent, (((0,), (0,)), ((), ())), preferred_element_type=jnp.float32
    )
    term_output = term_output.astype(jnp.bfloat16).astype(jnp.float32)
    grad_output = lax.psum_scatter(
        term_output.astype(jnp.bfloat16), "fsdp", scatter_dimension=1, tiled=True
    )
    projection_gradient = attend_backward(saved, attention_gradient)
    d_query_part = projection_gradient[:, :query_cols]
    d_keyvalue_part = projection_gradient[:, query_cols:]
    columns = tokens
    grad_query = lax.psum_scatter(
        lax.dot_general(
            columns, d_query_part, (((0,), (0,)), ((), ())), preferred_element_type=jnp.float32
        ).astype(jnp.bfloat16),
        "fsdp",
        scatter_dimension=0,
        tiled=True,
    )
    columns = tokens
    keyvalue = lax.psum_scatter(
        lax.dot_general(
            columns, d_keyvalue_part, (((0,), (0,)), ((), ())), preferred_element_type=jnp.float32
        ).astype(jnp.bfloat16),
        "fsdp",
        scatter_dimension=0,
        tiled=True,
    ).astype(jnp.float32)
    grad_key = keyvalue[:, :key_cols]
    grad_value = keyvalue[:, key_cols:]
    synced = outer_sync(snapshot, global_output, momentum, w_output)
    merged_output, global_new, momentum_new = synced
    return (
        block_out,
        grad_query[None],
        grad_key.astype(jnp.bfloat16)[None],
        grad_value.astype(jnp.bfloat16)[None],
        grad_output[None],
        merged_output,
        global_new,
        momentum_new,
    )


def solution(mesh):
    in_specs = (
        P(("replica", "fsdp"), None),
        P(("replica", "fsdp"), None),
        P("replica", "fsdp", None),
        P("replica", "fsdp", None),
        P("replica", "fsdp", None),
        P("replica", None, "fsdp"),
        P("replica", None, "fsdp"),
        P("replica", "fsdp"),
        P("replica", "fsdp"),
    )
    out_specs = (
        P(("replica", "fsdp"), None),
        P("replica", "fsdp", None),
        P("replica", "fsdp", None),
        P("replica", "fsdp", None),
        P("replica", None, "fsdp"),
        P("replica", None, "fsdp"),
        P("replica", "fsdp"),
        P("replica", "fsdp"),
    )
    return jax.shard_map(
        per_device, mesh=mesh, in_specs=in_specs, out_specs=out_specs, check_vma=False
    )
```

profile of v0, /device:TPU:0, one launch (start us, length us, event | category | flops | bytes accessed | tf_op | source)
XLA Modules:
  0.0 844.0 jit_solution(13855417262580166574)
XLA Ops:
  9.5 4.2 bitcast_convert_fusion
  17.3 41.8 %all-gather.12.cloned.1.call-done = bf16[1,2048,512]{2,1,0:T(8,128)(2,1)} async-done(((bf16[1,512,512]{2,1,0:T(8,128)(2,1)}), bf16[1,2048,512]{2,1,0:T(8,128)(2,1)}) %all-gather.12.cloned.1.call-update) | async-done | bytes 2097168 | tf_op jit(solution)/shard_map/all_gather | solution.py:146
  63.0 42.4 %all-gather.14.cloned.1.call-done = bf16[1,2048,512]{2,1,0:T(8,128)(2,1)} async-done(((bf16[1,512,512]{2,1,0:T(8,128)(2,1)}), bf16[1,2048,512]{2,1,0:T(8,128)(2,1)}) %all-gather.14.cloned.1.call-update) | async-done | bytes 2097168 | tf_op jit(solution)/shard_map/all_gather | solution.py:141
  113.3 142.0 %all-gather.16.cloned.1.call-done = bf16[1,2048,2048]{2,1,0:T(8,128)(2,1)} async-done(((bf16[1,512,2048]{2,1,0:T(8,128)(2,1)}), bf16[1,2048,2048]{2,1,0:T(8,128)(2,1)}) %all-gather.16.cloned.1.call-update) | async-done | bytes 8388624 | tf_op jit(solution)/shard_map/all_gather | solution.py:136
  255.3 6.3 fusion.30
  265.7 138.9 %all-gather.18.cloned.1.call-done = bf16[1,2048,2048]{2,1,0:T(8,128)(2,1)} async-done(((bf16[1,2048,512]{2,1,0:T(8,128)(2,1)}), bf16[1,2048,2048]{2,1,0:T(8,128)(2,1)}) %all-gather.18.cloned.1.call-update) | async-done | bytes 8388624 | tf_op jit(solution)/shard_map/all_gather | solution.py:150
  404.6 10.1 %fusion.18 = bf16[384,2048]{1,0:T(8,128)(2,1)} fusion(bf16[384,2048]{1,0:T(8,128)(2,1)S(1)} %copy-done, bf16[1,2048,2048]{2,1,0:T(8,128)(2,1)} %all-gather.18.cloned.1.call-done), kind=kOutput, calls=%fused_computation.30 | convolution fusion | flops 3222011904 | bytes 11534336 | tf_op jit(solution)/shard_map/dot_general | solution.py:154
  417.5 10.0 %fusion.62 = (f32[4,4,384]{2,1,0:T(4,128)}, f32[4,4,384,384]{2,3,1,0:T(8,128)}) fusion(pred[384,384]{0,1:T(8,128)(4,1)} %iota_compare_fusion, bf16[384,4,64]{2,0,1:T(8,128)(2,1)} %get-tuple-element.33, bf16[384,4,64]{2,0,1:T(8,128)(2,1)} %get-tuple-element.32, bf16[384,4,4,64]{3,0,2,1:T(8,128)(2,1)S(1)} %bitcast.126, bf16[384,4,4,64]{3,0,2,1:T(8,128)(2,1)} %bitcast.128), kind=kOutput, calls=%fused_computation.83 | convolution fusion | flops 617349504 | bytes 11575296 | tf_op jit(solution)/shard_map/sub | solution.py:56
  427.4 9.9 %fusion.1 = (f32[4,4,384]{2,1,0:T(4,128)}, f32[4,384,384,4]{2,1,3,0:T(8,128)}) fusion(f32[4,4,384,384]{2,3,1,0:T(8,128)} %get-tuple-element.44, f32[4,4,384]{2,1,0:T(4,128)} %get-tuple-element.43, bf16[384,4,4,128]{0,3,2,1:T(8,128)(2,1)} %bitcast.131, bf16[384,4,128,1]{2,1,0,3:T(4,128)(2,1)} %bitcast.134), kind=kOutput, calls=%fused_computation.3 | convolution fusion | flops 611051520 | bytes 20889600 | tf_op jit(solution)/shard_map/qkgd,skd->kgqs/dot_general | solution.py:75
  437.3 10.1 %fusion.3 = bf16[4,4,384,384]{2,3,1,0:T(8,128)(2,1)} fusion(f32[4,384,384,4]{2,1,3,0:T(8,128)} %get-tuple-element.46, f32[4,4,384]{2,1,0:T(4,128)} %get-tuple-element.45, f32[4,4,384,384]{2,3,1,0:T(8,128)} %get-tuple-element.44, f32[4,4,384]{2,1,0:T(4,128)} %get-tuple-element.43), kind=kLoop, calls=%fused_computation.5 | loop fusion | flops 9437184 | bytes 23642112 | tf_op jit(solution)/shard_map/convert_element_type | solution.py:78
  447.5 4.3 fusion.42
  455.0 5.3 fusion.43
  460.4 4.3 convert_bitcast_fusion.1
  465.8 3.5 convolution_multiply_fusion
  476.4 3.7 subtract_convert_fusion
  481.4 6.9 convert_bitcast_fusion
  489.4 4.9 fusion.33
  495.4 6.8 convolution_convert_fusion
  503.6 8.6 %add_convert_fusion.1 = bf16[384,2048]{1,0:T(8,128)(2,1)} fusion(bf16[384,2048]{1,0:T(8,128)(2,1)S(1)} %copy-done.11, bf16[384,2048]{0,1:T(8,128)(2,1)} %bitcast.139, bf16[1,2048,2048]{2,1,0:T(8,128)(2,1)} %all-gather.18.cloned.1.call-done), kind=kOutput, calls=%fused_computation.27 | convolution fusion | flops 3223584768 | bytes 13107200 | tf_op jit(solution)/shard_map/dot_general | solution.py:152
  512.2 4.9 fusion.25
  517.1 23.5 %reduce-scatter.7.cloned.1.call-done = bf16[512,1024]{0,1:T(8,128)(2,1)} async-done(((bf16[2048,1024]{0,1:T(8,128)(2,1)}), bf16[512,1024]{0,1:T(8,128)(2,1)}) %reduce-scatter.7.cloned.1.call-update) | async-done | bytes 1048592 | tf_op jit(solution)/shard_map/reduce_scatter | solution.py:177
  543.9 144.1 %reduce-scatter.5.cloned.1.call-done = bf16[512,2048]{0,1:T(8,128)(2,1)} async-done(((bf16[2048,2048]{0,1:T(8,128)(2,1)}), bf16[512,2048]{0,1:T(8,128)(2,1)}) %reduce-scatter.5.cloned.1.call-update) | async-done | bytes 2097168 | tf_op jit(solution)/shard_map/reduce_scatter | solution.py:168
  687.9 3.9 copy.55
  691.9 144.3 %reduce-scatter.9.cloned.1.call-done = bf16[2048,512]{1,0:T(8,128)(2,1)} async-done(((bf16[2048,2048]{1,0:T(8,128)(2,1)}), bf16[2048,512]{1,0:T(8,128)(2,1)}) %reduce-scatter.9.cloned.1.call-update) | async-done | bytes 2097168 | tf_op jit(solution)/shard_map/reduce_scatter | solution.py:161
  (72 shorter events, 43.2 us)
Async XLA Ops:
  8.0 396.6 %copy-start = (bf16[384,2048]{1,0:T(8,128)(2,1)S(1)}, bf16[384,2048]{1,0:T(8,128)(2,1)}, u32[]{:S(2)}) copy-start(bf16[384,2048]{1,0:T(8,128)(2,1)} %param.10) | copy-start | bytes 4718596
  8.0 51.1 %all-gather.12.cloned.1.call-start = ((), (), s32[]{:S(2)}) async-start(), calls=%async_computation.9 | async-start | bytes 2621440 | tf_op jit(solution)/shard_map/all_gather | solution.py:146
  8.7 96.6 %all-gather.14.cloned.1.call-start = ((), (), s32[]{:S(2)}) async-start(), calls=%async_computation.10 | async-start | bytes 2621440 | tf_op jit(solution)/shard_map/all_gather | solution.py:141
  9.5 101.2 %reduce-scatter.11.cloned.1.call-start = ((), (), s32[]{:S(2)}) async-start(), calls=%async_computation.7 | async-start | bytes 4718592 | tf_op jit(solution)/shard_map/reduce_scatter | solution.py:106
  13.8 241.5 %all-gather.16.cloned.1.call-start = ((), (), s32[]{:S(2)}) async-start(), calls=%async_computation.11 | async-start | bytes 10485760 | tf_op jit(solution)/shard_map/all_gather | solution.py:136
  14.5 390.1 %all-gather.18.cloned.1.call-start = ((), (), s32[]{:S(2)}) async-start(), calls=%async_computation.12 | async-start | bytes 10485760 | tf_op jit(solution)/shard_map/all_gather | solution.py:150
  15.1 497.1 %all-gather.10.cloned.1.call-start = ((), (), s32[]{:S(2)}) async-start(), calls=%async_computation.8 | async-start | bytes 4718592 | tf_op jit(solution)/shard_map/all_gather | solution.py:113
  108.7 0.9 copy-start.1
  113.3 427.3 %reduce-scatter.7.cloned.1.call-start = ((), (), s32[]{:S(2)}) async-start(), calls=%async_computation.5 | async-start | bytes 5242880 | tf_op jit(solution)/shard_map/reduce_scatter | solution.py:177
  261.6 1.0 copy-start.2
  451.8 3.3 copy-start.5
  455.0 5.4 copy-start.7
  455.0 5.4 copy-start.9
  464.7 1.0 copy-start.3
  464.7 1.1 copy-start.4
  464.8 223.2 %reduce-scatter.5.cloned.1.call-start = ((), (), s32[]{:S(2)}) async-start(), calls=%async_computation.4 | async-start | bytes 10485760 | tf_op jit(solution)/shard_map/reduce_scatter | solution.py:168
  480.0 1.4 copy-start.10
  488.4 1.0 copy-start.6
  488.4 1.0 copy-start.8
  488.4 347.7 %reduce-scatter.9.cloned.1.call-start = ((), (), s32[]{:S(2)}) async-start(), calls=%async_computation.6 | async-start | bytes 10485760 | tf_op jit(solution)/shard_map/reduce_scatter | solution.py:161
  494.3 1.1 copy-start.12
  502.2 1.4 copy-start.11
Sparse Core Ops, SparseCore 0:
  10.4 48.6 all-gather.11
  60.6 44.6 all-gather.13
  106.9 148.3 all-gather.15
  256.7 147.8 all-gather.17
  407.1 34.8 all-gather.9
  464.9 75.6 reduce-scatter.6
  542.9 144.9 reduce-scatter.4
  690.9 145.1 reduce-scatter.8
Sparse Core Ops, SparseCore 1:
  13.8 53.9 reduce-scatter.10
where the time goes:
time: 852 us; the launch traced here: 844 us
  waiting for transfers between devices  680 us (80%)
  matrix products  86.9 us (10%)
  other arithmetic  32.1 us (4%)
  local copies, waits for them, and re-layouts  28.4 us (3%)
  between operations  16.2 us (2%)
    reduce_scatter x1, waiting for transfers between devices, per_device(): lax.psum_scatter(term_output.astype(jnp.bfloat16), 'fsdp', scatter_dimens...  144 us
    reduce_scatter x1, waiting for transfers between devices, per_device(): lax.psum_scatter(lax.dot_general(columns, d_query_part, (((0,), (0,)), ((...  144 us
    all_gather x1, waiting for transfers between devices, per_device(): lax.all_gather(w_query[0], 'fsdp', axis=0, tiled=True)  142 us
    all_gather x1, waiting for transfers between devices, per_device(): whole_output = lax.all_gather(w_output[0], 'fsdp', axis=1, tiled=True)  139 us
    all_gather x1, waiting for transfers between devices, per_device(): lax.all_gather(replica_key_weight[0], 'fsdp', axis=0, tiled=True)  42.4 us
    all_gather x1, waiting for transfers between devices, per_device(): lax.all_gather(replica_value_weight[0], 'fsdp', axis=0, tiled=True)  41.8 us
    reduce_scatter x1, waiting for transfers between devices, per_device(): lax.psum_scatter(lax.dot_general(columns, d_keyvalue_part, (((0,), (0,)),...  23.5 us
    unnamed x32, local copies, waits for them, and re-layouts  17.6 us
  transfers between devices with their start and end apart: 9, of which 7 were waited for; matrix products, arithmetic and copies ran while one was open for 17% of the time, Pallas kernels for 0%

commit v1 on v0

v1 whole, which is shorter than its diff:
```python
import jax
import jax.numpy as jnp
from jax import lax
from jax.sharding import PartitionSpec as P

HEAD_SIZE = 128
QUERY_HEADS = 16
KEYVALUE_HEADS = 4


theta_base = 500000.0
momentum_decay = 0.9
outer_rate = 0.7
mixing = 0.5


def apply_rotation(value_rows, sign):
    sequence_length = value_rows.shape[0]
    half = value_rows.shape[2] // 2
    position = jnp.arange(sequence_length).astype(jnp.float32)
    freq = jnp.exp(
        -jnp.log(theta_base) * jnp.arange(half).astype(jnp.float32) * 2.0 / value_rows.shape[2]
    )
    angle = position[:, None] * freq[None, :]
    cosine = jnp.cos(angle)[:, None, :]
    sine = sign * jnp.sin(angle)[:, None, :]
    first = value_rows[..., :half]
    second = value_rows[..., half:]
    return jnp.concatenate(
        [first * cosine - second * sine, first * sine + second * cosine], axis=-1
    )


def rotate(value_rows, sign):
    return jax.vmap(lambda rows: apply_rotation(rows, sign))(value_rows)


def gather(block):
    return lax.all_gather(block, "fsdp", axis=0, tiled=True)


def attend(query_raw, key_raw, value_raw):
    scale = HEAD_SIZE ** (-0.5)
    query_rows = rotate(query_raw, 1.0).astype(jnp.bfloat16)
    key_rows = rotate(key_raw[:, :, None, :], 1.0)[:, :, 0].astype(jnp.bfloat16)
    value_rows = value_raw.astype(jnp.bfloat16)
    length = query_raw.shape[1]
    scores = (
        jnp.einsum("sqgd,skd->sgqk", query_rows, key_rows, preferred_element_type=jnp.float32)
        * scale
    )
    causal = jnp.arange(length)[:, None] >= jnp.arange(length)[None, :]
    scores = jnp.where(causal, scores, -1e30)
    top = jnp.max(scores, axis=-1, keepdims=True)
    expo = jnp.exp(scores - top)
    probs = expo / jnp.sum(expo, axis=-1, keepdims=True)
    probs_b = probs.astype(jnp.bfloat16)
    attn = jnp.einsum("sgqk,skd->sqgd", probs_b, value_rows, preferred_element_type=jnp.float32)
    return attn.astype(jnp.bfloat16), (query_rows, key_rows, value_rows, probs, probs_b)


def attend_gradient(saved, d_attn):
    query_rows, key_rows, value_rows, probs, probs_b = saved
    scale = HEAD_SIZE ** (-0.5)
    d_values = jnp.einsum("sgqk,sqgd->skd", probs_b, d_attn, preferred_element_type=jnp.float32)
    d_probs = jnp.einsum("sqgd,skd->sgqk", d_attn, value_rows, preferred_element_type=jnp.float32)
    d_scores = (probs * (d_probs - jnp.sum(d_probs * probs, axis=-1, keepdims=True))).astype(
        jnp.bfloat16
    )
    d_queries = (
        jnp.einsum("sgqk,skd->sqgd", d_scores, key_rows, preferred_element_type=jnp.float32) * scale
    )
    d_keys = (
        jnp.einsum("sgqk,sqgd->skd", d_scores, query_rows, preferred_element_type=jnp.float32)
        * scale
    )
    d_queries = rotate(d_queries, -1.0)
    d_keys = rotate(d_keys[:, :, None, :], -1.0)[:, :, 0]
    rows = d_attn.shape[0] * d_attn.shape[1]
    return jnp.concatenate(
        [part.astype(jnp.bfloat16).reshape(rows, -1) for part in (d_queries, d_keys, d_values)],
        axis=1,
    )


def exchange(pick, place, out):
    n = lax.axis_size("fsdp")
    me = lax.axis_index("fsdp")
    out = place(out, pick(me), me)
    for shift in range(1, n):
        pairs = [(f, (f + shift) % n) for f in range(n)]
        piece = lax.ppermute(pick(lax.rem(me + shift, n)), "fsdp", pairs)
        out = place(out, piece, lax.rem(me + n - shift, n))
    return out


def outer_sync(snapshot, global_output, momentum, w_output):
    total = lax.psum_scatter(
        snapshot[0].astype(jnp.float32), "replica", scatter_dimension=0, tiled=True
    )
    mean_snapshot = total / lax.axis_size("replica")
    delta = global_output - mean_snapshot
    momentum_new = momentum_decay * momentum + delta
    global_new = global_output - outer_rate * (delta + momentum_decay * momentum_new)
    gathered = lax.all_gather(global_new, "replica", axis=0, tiled=True)
    merged = (mixing * w_output[0].astype(jnp.float32) + (1.0 - mixing) * gathered).astype(
        jnp.bfloat16
    )
    return (merged[None], global_new, momentum_new)


def per_device(
    tokens,
    cotangent,
    w_query,
    replica_key_weight,
    replica_value_weight,
    w_output,
    snapshot,
    global_output,
    momentum,
):
    n = lax.axis_size("fsdp")
    me = lax.axis_index("fsdp")
    length, width = tokens.shape
    depth = w_query.shape[1]
    own_query = w_query.shape[2] // n
    own_key = replica_key_weight.shape[2] // n
    own_cols = own_query + 2 * own_key
    group = own_query // HEAD_SIZE
    model_cols = w_output.shape[2]
    total_rows = n * length

    all_tokens = gather(tokens)
    all_cotangent = gather(cotangent)

    def pick_weight(d):
        return jnp.concatenate(
            [
                lax.dynamic_slice_in_dim(w_query[0], d * own_query, own_query, 1),
                lax.dynamic_slice_in_dim(replica_key_weight[0], d * own_key, own_key, 1),
                lax.dynamic_slice_in_dim(replica_value_weight[0], d * own_key, own_key, 1),
            ],
            axis=1,
        )

    def place_rows(out, piece, f):
        return lax.dynamic_update_slice_in_dim(out, piece, f * piece.shape[0], 0)

    def place_cols(out, piece, f):
        return lax.dynamic_update_slice_in_dim(out, piece, f * piece.shape[1], 1)

    w_in = exchange(pick_weight, place_rows, jnp.zeros((n * depth, own_cols), jnp.bfloat16))
    w_out_rows = exchange(
        lambda d: lax.dynamic_slice_in_dim(w_output[0], d * own_query, own_query, 0),
        place_cols,
        jnp.zeros((own_query, n * model_cols), jnp.bfloat16),
    )

    raw = jnp.dot(all_tokens, w_in, preferred_element_type=jnp.float32)
    query_raw = raw[:, :own_query].reshape(n, length, group, HEAD_SIZE)
    key_raw = raw[:, own_query : own_query + own_key].reshape(n, length, HEAD_SIZE)
    value_raw = raw[:, own_query + own_key :].reshape(n, length, HEAD_SIZE)
    attn, saved = attend(query_raw, key_raw, value_raw)

    own_attn = attn.reshape(total_rows, own_query)
    all_attn = lax.all_gather(own_attn, "fsdp", axis=1, tiled=True)

    d_attn = (
        lax.dot_general(
            all_cotangent,
            w_out_rows,
            (((1,), (1,)), ((), ())),
            preferred_element_type=jnp.float32,
        )
        .astype(jnp.bfloat16)
        .reshape(n, length, group, HEAD_SIZE)
    )
    d_in = attend_gradient(saved, d_attn)
    grad_in = lax.dot_general(
        all_tokens, d_in, (((0,), (0,)), ((), ())), preferred_element_type=jnp.float32
    ).astype(jnp.bfloat16)

    def place_grads(outs, piece, f):
        grad_query, grad_key, grad_value = outs
        return (
            place_cols(grad_query, piece[:, :own_query], f),
            place_cols(grad_key, piece[:, own_query : own_query + own_key], f),
            place_cols(grad_value, piece[:, own_query + own_key :], f),
        )

    grad_query, grad_key, grad_value = exchange(
        lambda d: lax.dynamic_slice_in_dim(grad_in, d * depth, depth, 0),
        place_grads,
        tuple(
            jnp.zeros(w.shape[1:], jnp.bfloat16)
            for w in (w_query, replica_key_weight, replica_value_weight)
        ),
    )

    own_token_cols = lax.dynamic_slice_in_dim(all_tokens, me * model_cols, model_cols, 1)
    out_cols = (
        own_token_cols.astype(jnp.float32)
        + jnp.dot(all_attn, w_output[0], preferred_element_type=jnp.float32)
    ).astype(jnp.bfloat16)
    block_out = exchange(
        lambda d: lax.dynamic_slice_in_dim(out_cols, d * length, length, 0),
        place_cols,
        jnp.zeros((length, width), jnp.bfloat16),
    )
    own_cotangent_cols = lax.dynamic_slice_in_dim(all_cotangent, me * model_cols, model_cols, 1)
    grad_output = lax.dot_general(
        all_attn, own_cotangent_cols, (((0,), (0,)), ((), ())), preferred_element_type=jnp.float32
    ).astype(jnp.bfloat16)

    merged_output, global_new, momentum_new = outer_sync(
        snapshot, global_output, momentum, w_output
    )
    return (
        block_out,
        grad_query[None],
        grad_key[None],
        grad_value[None],
        grad_output[None],
        merged_output,
        global_new,
        momentum_new,
    )


def solution(mesh):
    in_specs = (
        P(("replica", "fsdp"), None),
        P(("replica", "fsdp"), None),
        P("replica", "fsdp", None),
        P("replica", "fsdp", None),
        P("replica", "fsdp", None),
        P("replica", None, "fsdp"),
        P("replica", None, "fsdp"),
        P("replica", "fsdp"),
        P("replica", "fsdp"),
    )
    out_specs = (
        P(("replica", "fsdp"), None),
        P("replica", "fsdp", None),
        P("replica", "fsdp", None),
        P("replica", "fsdp", None),
        P("replica", None, "fsdp"),
        P("replica", None, "fsdp"),
        P("replica", "fsdp"),
        P("replica", "fsdp"),
    )
    return jax.shard_map(
        per_device, mesh=mesh, in_specs=in_specs, out_specs=out_specs, check_vma=False
    )
```

time: 852 us -> 650 us (0.76)
  waiting for transfers between devices: 680 us -> 417 us
  local copies, waits for them, and re-layouts: 28.4 us -> 72.4 us
  starting transfers between devices: 0.83 us -> 32.2 us
  matrix products: 86.9 us -> 63.3 us
    reduce_scatter x3 -> x0, waiting for transfers between devices: 312 us -> none  [the longest x1 144 us: per_device(): lax.psum_scatter(term_output.astype(jnp.bfloat16), 'fsdp', scatter_dimens...]
    ppermute x0 -> x12, waiting for transfers between devices: none -> 266 us  [exchange(): piece = lax.ppermute(pick(lax.rem(me + shift, n)), 'fsdp', pairs)]
    all_gather x4 -> x3, waiting for transfers between devices: 365 us -> 114 us  [the longest x2 87.8 us: gather(): return lax.all_gather(block, 'fsdp', axis=0, tiled=True)]
    reduce_scatter x1, waiting for transfers between devices: 0.01 us -> 36 us  [outer_sync(): lax.psum_scatter(snapshot[0].astype(jnp.float32), 'replica', scatter_dime...]
    ppermute x0 -> x12, starting transfers between devices: none -> 32 us  [exchange(): piece = lax.ppermute(pick(lax.rem(me + shift, n)), 'fsdp', pairs)]
    dot_general x13 -> x10, matrix products: 77 us -> 53.4 us  [the longest x1 8.01 us: per_device(): lax.dot_general(all_cotangent, w_out_rows, (((1,), (1,)), ((), ())), pref...]
    dynamic_update_slice x0 -> x22, local copies, waits for them, and re-layouts: none -> 18.4 us  [the longest x19 14.2 us: place_cols(): return lax.dynamic_update_slice_in_dim(out, piece, f * piece.shape[1], 1)]
    broadcast_in_dim x1 -> x25, local copies, waits for them, and re-layouts: 1.27 us -> 10.8 us  [the longest x9 4.4 us: per_device(): grad_query[None]]
  transfers between devices with their start and end apart: 9 -> 17, of which waited for: 7 -> 11; matrix products, arithmetic and copies ran while one was open for 17% -> 24% of each run, Pallas kernels for 0% -> 0%
where the time goes in v1:
time: 650 us; the launch traced here: 640 us
  waiting for transfers between devices  417 us (64%)
  local copies, waits for them, and re-layouts  72.4 us (11%)
  matrix products  63.3 us (10%)
  other arithmetic  37.9 us (6%)
  starting transfers between devices  32.2 us (5%)
  between operations  16.7 us (3%)
    ppermute x12, waiting for transfers between devices, exchange(): piece = lax.ppermute(pick(lax.rem(me + shift, n)), 'fsdp', pairs)  266 us
    all_gather x2, waiting for transfers between devices, gather(): return lax.all_gather(block, 'fsdp', axis=0, tiled=True)  87.8 us
    reduce_scatter x1, waiting for transfers between devices, outer_sync(): lax.psum_scatter(snapshot[0].astype(jnp.float32), 'replica', scatter_dime...  36 us
    ppermute x12, starting transfers between devices, exchange(): piece = lax.ppermute(pick(lax.rem(me + shift, n)), 'fsdp', pairs)  32 us
    all_gather x1, waiting for transfers between devices, per_device(): all_attn = lax.all_gather(own_attn, 'fsdp', axis=1, tiled=True)  26.2 us
    dynamic_update_slice x19, local copies, waits for them, and re-layouts, place_cols(): return lax.dynamic_update_slice_in_dim(out, piece, f * piece.shape[1], 1)  14.2 us
    unnamed x70, local copies, waits for them, and re-layouts  13.5 us
  transfers between devices with their start and end apart: 17, of which 11 were waited for; matrix products, arithmetic and copies ran while one was open for 24% of the time, Pallas kernels for 0%

profile of v1, /device:TPU:0, one launch (start us, length us, event | category | flops | bytes accessed | tf_op | source)
XLA Modules:
  0.0 639.8 jit_solution(5933914558639544771)
XLA Ops:
  8.0 4.2 bitcast_convert_fusion
  30.4 36.0 %reduce-scatter.2.cloned.1.call-done = f32[256,512]{1,0:T(8,128)} async-done(((f32[2048,512]{1,0:T(8,128)}), f32[256,512]{1,0:T(8,128)}) %reduce-scatter.2.cloned.1.call-update) | async-done | bytes 524304 | tf_op jit(solution)/shard_map/reduce_scatter | solution.py:98
  70.5 35.6 %collective-permute-done.6 = bf16[512,512]{1,0:T(8,128)(2,1)} collective-permute-done((bf16[512,512]{1,0:T(8,128)(2,1)}, bf16[512,512]{1,0:T(8,128)(2,1)}, u32[]{:S(2)}, u32[]{:S(2)}) %collective-permute-start.6) | collective-permute-done | bytes 524320 | tf_op jit(solution)/shard_map/ppermute | solution.py:92
  110.3 71.0 %collective-permute-done.7 = bf16[512,512]{1,0:T(8,128)(2,1)} collective-permute-done((bf16[512,512]{1,0:T(8,128)(2,1)}, bf16[512,512]{1,0:T(8,128)(2,1)}, u32[]{:S(2)}, u32[]{:S(2)}) %collective-permute-start.7) | collective-permute-done | bytes 524320 | tf_op jit(solution)/shard_map/ppermute | solution.py:92
  186.6 49.4 %collective-permute-done.2 = bf16[512,768]{1,0:T(8,128)(2,1)} collective-permute-done((bf16[512,768]{1,0:T(8,128)(2,1)}, bf16[512,768]{1,0:T(8,128)(2,1)}, u32[]{:S(2)}, u32[]{:S(2)}) %collective-permute-start.2) | collective-permute-done | bytes 786464 | tf_op jit(solution)/shard_map/ppermute | solution.py:92
  237.3 7.2 %convolution_bitcast_fusion = f32[1536,768]{0,1:T(8,128)S(1)} fusion(bf16[2048,768]{1,0:T(8,128)(2,1)S(1)} %constant_dynamic-update-slice_fusion.18, bf16[1536,2048]{1,0:T(8,128)(2,1)} %all-gather.5.cloned.1.call-done), kind=kOutput, calls=%fused_computation.14 | convolution fusion | flops 4831838208 | bytes 14155776 | tf_op jit(solution)/shard_map/dot_general | solution.py:160
  264.3 87.8 %all-gather.9.cloned.1.call-done = bf16[1536,2048]{1,0:T(8,128)(2,1)} async-done(((bf16[384,2048]{1,0:T(8,128)(2,1)}), bf16[1536,2048]{1,0:T(8,128)(2,1)}) %all-gather.9.cloned.1.call-update) | async-done | bytes 6291472 | tf_op jit(solution)/shard_map/all_gather | solution.py:39
  352.1 8.0 %fusion.9 = bf16[1536,512]{0,1:T(8,128)(2,1)} fusion(bf16[512,2048]{1,0:T(8,128)(2,1)} %copy-done.6, bf16[1536,2048]{1,0:T(8,128)(2,1)} %all-gather.9.cloned.1.call-done), kind=kOutput, calls=%fused_computation.25 | convolution fusion | flops 3222011904 | bytes 9961472 | tf_op jit(solution)/shard_map/dot_general | solution.py:170
  370.7 4.5 subtract_convert_fusion.1
  375.2 9.9 %fusion.44 = (f32[4,4,384]{2,1,0:T(4,128)S(1)}, f32[4,4,384,384]{2,3,1,0:T(8,128)}) fusion(pred[384,384]{0,1:T(8,128)(4,1)} %iota_compare_fusion, bf16[4,384,1,64]{3,1,0,2:T(8,128)(2,1)} %get-tuple-element.34, bf16[4,384,1,64]{3,1,0,2:T(8,128)(2,1)} %get-tuple-element.33, bf16[4,384,4,64]{3,1,2,0:T(8,128)(2,1)} %get-tuple-element.11, ...), kind=kOutput, calls=%fused_computation.134 | convolution fusion | flops 617349504 | bytes 11575296 | tf_op jit(solution)/shard_map/sub | solution.py:55
  385.6 4.9 fusion.26
  393.9 7.0 %fusion.1 = (f32[4,4,384]{2,1,0:T(4,128)S(1)}, f32[4,384,384,4]{2,1,3,0:T(8,128)}) fusion(f32[4,4,384,384]{2,3,1,0:T(8,128)} %get-tuple-element.55, f32[4,4,384]{2,1,0:T(4,128)S(1)} %copy-done.23, bf16[4,384,128,1]{2,1,3,0:T(8,128)(2,1)S(1)} %copy-done.21, bf16[4,384,4,128]{3,1,2,0:T(8,128)(2,1)S(1)} %copy-done.12), kind=kOutput, calls=%fused_computation.3 | convolution fusion | flops 611051520 | bytes 20889600 | tf_op jit(solution)/shard_map/sqgd,skd->sgqk/dot_general | solution.py:66
  400.9 10.9 %fusion.3 = bf16[4,4,384,384]{2,3,1,0:T(8,128)(2,1)} fusion(f32[4,384,384,4]{2,1,3,0:T(8,128)} %get-tuple-element.57, f32[4,4,384]{2,1,0:T(4,128)S(1)} %get-tuple-element.56, f32[4,4,384,384]{2,3,1,0:T(8,128)} %get-tuple-element.55, f32[4,4,384]{2,1,0:T(4,128)S(1)} %copy-done.24), kind=kLoop, calls=%fused_computation.5 | loop fusion | flops 9437184 | bytes 23642112 | tf_op jit(solution)/shard_map/convert_element_type | solution.py:67
  411.9 4.2 multiply_bitcast_fusion
  425.7 6.2 convolution_convert_fusion
  441.9 30.7 %collective-permute-done.9 = bf16[512,768]{0,1:T(8,128)(2,1)S(1)} collective-permute-done((bf16[512,768]{0,1:T(8,128)(2,1)}, bf16[512,768]{0,1:T(8,128)(2,1)S(1)}, u32[]{:S(2)}, u32[]{:S(2)}) %collective-permute-start.9) | collective-permute-done | bytes 786464 | tf_op jit(solution)/shard_map/ppermute | solution.py:92
  472.8 57.5 %collective-permute-done.10 = bf16[512,768]{0,1:T(8,128)(2,1)S(1)} collective-permute-done((bf16[512,768]{0,1:T(8,128)(2,1)}, bf16[512,768]{0,1:T(8,128)(2,1)S(1)}, u32[]{:S(2)}, u32[]{:S(2)}) %collective-permute-start.10) | collective-permute-done | bytes 786464 | tf_op jit(solution)/shard_map/ppermute | solution.py:92
  531.0 4.6 collective-permute-done.11
  551.5 4.2 fusion.20
  555.7 26.2 %all-gather.7.cloned.1.call-done = bf16[1536,2048]{1,0:T(8,128)(2,1)} async-done(((bf16[1536,512]{1,0:T(8,128)(2,1)}), bf16[1536,2048]{1,0:T(8,128)(2,1)}) %all-gather.7.cloned.1.call-update) | async-done | bytes 6291472 | tf_op jit(solution)/shard_map/all_gather | solution.py:167
  581.9 6.8 %fusion.8 = bf16[1536,512]{1,0:T(8,128)(2,1)S(1)} fusion(bf16[1536,2048]{1,0:T(8,128)(2,1)} %all-gather.7.cloned.1.call-done, bf16[1,2048,512]{2,1,0:T(8,128)(2,1)S(1)} %copy-done.1, bf16[1536,2048]{1,0:T(8,128)(2,1)} %all-gather.5.cloned.1.call-done, s32[]{:T(128)S(6)} %select_n.28), kind=kOutput, calls=%fused_computation.22 | convolution fusion | flops 3223584768 | bytes 11534340 | tf_op jit(solution)/shard_map/dot_general | solution.py:204
  589.1 15.6 %collective-permute-start.3 = (bf16[384,512]{1,0:T(8,128)(2,1)S(1)}, bf16[384,512]{1,0:T(8,128)(2,1)S(1)}, u32[]{:S(2)}, u32[]{:S(2)}) collective-permute-start(bf16[384,512]{1,0:T(8,128)(2,1)S(1)} %get-tuple-element.29), channel_id=1, source_target_pairs={{0,1},{1,2},{2,3},{3,0},{4,5},{5,6},{6,7},{7,4},{8,9},{9,10},{10,1... | collective-permute-start | bytes 1179656 | tf_op jit(solution)/shard_map/ppermute | solution.py:92
  607.2 6.0 fusion.10
  615.9 14.8 %collective-permute-done.4 = bf16[384,512]{1,0:T(8,128)(2,1)S(1)} collective-permute-done((bf16[384,512]{1,0:T(8,128)(2,1)S(1)}, bf16[384,512]{1,0:T(8,128)(2,1)S(1)}, u32[]{:S(2)}, u32[]{:S(2)}) %collective-permute-start.4) | collective-permute-done | bytes 393248 | tf_op jit(solution)/shard_map/ppermute | solution.py:92
  (182 shorter events, 109.7 us)
Async XLA Ops:
  8.0 58.4 %reduce-scatter.2.cloned.1.call-start = ((), (), s32[]{:S(2)}) async-start(), calls=%async_computation.4 | async-start | bytes 4718592 | tf_op jit(solution)/shard_map/reduce_scatter | solution.py:98
  12.3 225.0 %all-gather.5.cloned.1.call-start = ((), (), s32[]{:S(2)}) async-start(), calls=%async_computation.1 | async-start | bytes 7864320 | tf_op jit(solution)/shard_map/all_gather | solution.py:39
  12.8 339.2 %all-gather.9.cloned.1.call-start = ((), (), s32[]{:S(2)}) async-start(), calls=%async_computation.3 | async-start | bytes 7864320 | tf_op jit(solution)/shard_map/all_gather | solution.py:39
  13.4 538.0 %all-gather.11.cloned.1.call-start = ((), (), s32[]{:S(2)}) async-start(), calls=%async_computation.5 | async-start | bytes 4718592 | tf_op jit(solution)/shard_map/all_gather | solution.py:105
  16.4 167.2 %collective-permute-start = (bf16[512,768]{1,0:T(8,128)(2,1)}, bf16[512,768]{1,0:T(8,128)(2,1)}, u32[]{:S(2)}, u32[]{:S(2)}) collective-permute-start(bf16[512,768]{1,0:T(8,128)(2,1)} %pad_maximum_fusion.2), channel_id=1, source_target_pairs={{0,1},{1,2},{2,3},{3,0},{4,5},{5,6},{6,7},{7,4},{8,9},{9,10},{10,1... | collective-permute-start | bytes 2359304 | tf_op jit(solution)/shard_map/ppermute | solution.py:92
  20.4 46.0 %copy-start.16 = (f32[256,512]{1,0:T(8,128)S(1)}, f32[256,512]{1,0:T(8,128)}, u32[]{:S(2)}) copy-start(f32[256,512]{1,0:T(8,128)} %param.16) | copy-start | bytes 1572868
  20.4 165.0 %collective-permute-start.1 = (bf16[512,768]{1,0:T(8,128)(2,1)}, bf16[512,768]{1,0:T(8,128)(2,1)}, u32[]{:S(2)}, u32[]{:S(2)}) collective-permute-start(bf16[512,768]{1,0:T(8,128)(2,1)} %pad_maximum_fusion.3), channel_id=1, source_target_pairs={{0,2},{1,3},{2,0},{3,1},{4,6},{5,7},{6,4},{7,5},{8,10},{9,11},{10,... | collective-permute-start | bytes 2359304 | tf_op jit(solution)/shard_map/ppermute | solution.py:92
  24.2 81.9 %collective-permute-start.6 = (bf16[512,512]{1,0:T(8,128)(2,1)}, bf16[512,512]{1,0:T(8,128)(2,1)}, u32[]{:S(2)}, u32[]{:S(2)}) collective-permute-start(bf16[512,512]{1,0:T(8,128)(2,1)} %get-tuple-element.21), channel_id=1, source_target_pairs={{0,1},{1,2},{2,3},{3,0},{4,5},{5,6},{6,7},{7,4},{8,9},{9,10},{10,1... | collective-permute-start | bytes 1572872 | tf_op jit(solution)/shard_map/ppermute | solution.py:92
  24.2 157.2 %collective-permute-start.7 = (bf16[512,512]{1,0:T(8,128)(2,1)}, bf16[512,512]{1,0:T(8,128)(2,1)}, u32[]{:S(2)}, u32[]{:S(2)}) collective-permute-start(bf16[512,512]{1,0:T(8,128)(2,1)} %get-tuple-element.22), channel_id=1, source_target_pairs={{0,2},{1,3},{2,0},{3,1},{4,6},{5,7},{6,4},{7,5},{8,10},{9,11},{10,... | collective-permute-start | bytes 1572872 | tf_op jit(solution)/shard_map/ppermute | solution.py:92
  26.1 156.4 %collective-permute-start.8 = (bf16[512,512]{1,0:T(8,128)(2,1)}, bf16[512,512]{1,0:T(8,128)(2,1)}, u32[]{:S(2)}, u32[]{:S(2)}) collective-permute-start(bf16[512,512]{1,0:T(8,128)(2,1)} %get-tuple-element.20), channel_id=1, source_target_pairs={{0,3},{1,0},{2,1},{3,2},{4,7},{5,4},{6,5},{7,6},{8,11},{9,8},{10,9... | collective-permute-start | bytes 1572872 | tf_op jit(solution)/shard_map/ppermute | solution.py:92
  68.8 513.1 %all-gather.7.cloned.1.call-start = ((), (), s32[]{:S(2)}) async-start(), calls=%async_computation.2 | async-start | bytes 7864320 | tf_op jit(solution)/shard_map/all_gather | solution.py:167
  106.1 130.0 %collective-permute-start.2 = (bf16[512,768]{1,0:T(8,128)(2,1)}, bf16[512,768]{1,0:T(8,128)(2,1)}, u32[]{:S(2)}, u32[]{:S(2)}) collective-permute-start(bf16[512,768]{1,0:T(8,128)(2,1)} %pad_maximum_fusion.4), channel_id=1, source_target_pairs={{0,3},{1,0},{2,1},{3,2},{4,7},{5,4},{6,5},{7,6},{8,11},{9,8},{10,9... | collective-permute-start | bytes 2359304 | tf_op jit(solution)/shard_map/ppermute | solution.py:92
  375.2 10.5 %copy-start.20 = (bf16[4,384,128,1]{2,1,3,0:T(8,128)(2,1)S(1)}, bf16[4,384,128,1]{2,1,3,0:T(8,128)(2,1)}, u32[]{:S(2)}) copy-start(bf16[4,384,128,1]{2,1,3,0:T(8,128)(2,1)} %copy.76) | copy-start | bytes 1179652
  400.9 11.0 %copy-start.10 = (bf16[4,384,1,64]{3,1,0,2:T(8,128)(2,1)S(1)}, bf16[4,384,1,64]{3,1,0,2:T(8,128)(2,1)}, u32[]{:S(2)}) copy-start(bf16[4,384,1,64]{3,1,0,2:T(8,128)(2,1)} %get-tuple-element.33) | copy-start | bytes 589828
  400.9 11.0 %copy-start.11 = (bf16[4,384,1,64]{3,1,0,2:T(8,128)(2,1)S(1)}, bf16[4,384,1,64]{3,1,0,2:T(8,128)(2,1)}, u32[]{:S(2)}) copy-start(bf16[4,384,1,64]{3,1,0,2:T(8,128)(2,1)} %get-tuple-element.34) | copy-start | bytes 589828
  433.4 39.2 %collective-permute-start.9 = (bf16[512,768]{0,1:T(8,128)(2,1)}, bf16[512,768]{0,1:T(8,128)(2,1)S(1)}, u32[]{:S(2)}, u32[]{:S(2)}) collective-permute-start(bf16[512,768]{0,1:T(8,128)(2,1)} %get-tuple-element.16), channel_id=1, source_target_pairs={{0,1},{1,2},{2,3},{3,0},{4,5},{5,6},{6,7},{7,4},{8,9},{9,10},{10,1... | collective-permute-start | bytes 2359304 | tf_op jit(solution)/shard_map/ppermute | solution.py:92
  433.6 96.7 %collective-permute-start.10 = (bf16[512,768]{0,1:T(8,128)(2,1)}, bf16[512,768]{0,1:T(8,128)(2,1)S(1)}, u32[]{:S(2)}, u32[]{:S(2)}) collective-permute-start(bf16[512,768]{0,1:T(8,128)(2,1)} %get-tuple-element.15), channel_id=1, source_target_pairs={{0,2},{1,3},{2,0},{3,1},{4,6},{5,7},{6,4},{7,5},{8,10},{9,11},{10,... | collective-permute-start | bytes 2359304 | tf_op jit(solution)/shard_map/ppermute | solution.py:92
  434.6 101.0 %collective-permute-start.11 = (bf16[512,768]{0,1:T(8,128)(2,1)}, bf16[512,768]{0,1:T(8,128)(2,1)}, u32[]{:S(2)}, u32[]{:S(2)}) collective-permute-start(bf16[512,768]{0,1:T(8,128)(2,1)} %get-tuple-element.14), channel_id=1, source_target_pairs={{0,3},{1,0},{2,1},{3,2},{4,7},{5,4},{6,5},{7,6},{8,11},{9,8},{10,9... | collective-permute-start | bytes 2359304 | tf_op jit(solution)/shard_map/ppermute | solution.py:92
  439.5 91.5 %copy-start.17 = (bf16[1,512,512]{2,1,0:T(8,128)(2,1)}, bf16[1,512,512]{2,1,0:T(8,128)(2,1)S(1)}, u32[]{:S(2)}) copy-start(bf16[1,512,512]{2,1,0:T(8,128)(2,1)S(1)} %constant_dynamic-update-slice_fusion.6) | copy-start | bytes 1572868
  542.3 9.2 %copy-start.1 = (bf16[1,2048,512]{2,1,0:T(8,128)(2,1)S(1)}, bf16[1,2048,512]{2,1,0:T(8,128)(2,1)}, u32[]{:S(2)}) copy-start(bf16[1,2048,512]{2,1,0:T(8,128)(2,1)} %param.14) | copy-start | bytes 6291460
  581.9 25.3 %copy-start.25 = (bf16[1536,2048]{1,0:T(8,128)(2,1)S(1)}, bf16[1536,2048]{1,0:T(8,128)(2,1)}, u32[]{:S(2)}) copy-start(bf16[1536,2048]{1,0:T(8,128)(2,1)} %all-gather.7.cloned.1.call-done) | copy-start | bytes 18874372
  589.1 26.7 %collective-permute-start.3 = (bf16[384,512]{1,0:T(8,128)(2,1)S(1)}, bf16[384,512]{1,0:T(8,128)(2,1)S(1)}, u32[]{:S(2)}, u32[]{:S(2)}) collective-permute-start(bf16[384,512]{1,0:T(8,128)(2,1)S(1)} %get-tuple-element.29), channel_id=1, source_target_pairs={{0,1},{1,2},{2,3},{3,0},{4,5},{5,6},{6,7},{7,4},{8,9},{9,10},{10,1... | collective-permute-start | bytes 1179656 | tf_op jit(solution)/shard_map/ppermute | solution.py:92
  604.8 25.8 %collective-permute-start.4 = (bf16[384,512]{1,0:T(8,128)(2,1)S(1)}, bf16[384,512]{1,0:T(8,128)(2,1)S(1)}, u32[]{:S(2)}, u32[]{:S(2)}) collective-permute-start(bf16[384,512]{1,0:T(8,128)(2,1)S(1)} %get-tuple-element.28), channel_id=1, source_target_pairs={{0,2},{1,3},{2,0},{3,1},{4,6},{5,7},{6,4},{7,5},{8,10},{9,11},{10,... | collective-permute-start | bytes 1179656 | tf_op jit(solution)/shard_map/ppermute | solution.py:92
  606.2 24.5 %collective-permute-start.5 = (bf16[384,512]{1,0:T(8,128)(2,1)S(1)}, bf16[384,512]{1,0:T(8,128)(2,1)S(1)}, u32[]{:S(2)}, u32[]{:S(2)}) collective-permute-start(bf16[384,512]{1,0:T(8,128)(2,1)S(1)} %get-tuple-element.27), channel_id=1, source_target_pairs={{0,3},{1,0},{2,1},{3,2},{4,7},{5,4},{6,5},{7,6},{8,11},{9,8},{10,9... | collective-permute-start | bytes 1179656 | tf_op jit(solution)/shard_map/ppermute | solution.py:92
  (26 other events, 82.8 us)
Sparse Core Ops, SparseCore 0:
  12.4 53.9 reduce-scatter.1
Sparse Core Ops, SparseCore 1:
  14.3 210.7 all-gather.4
  226.5 125.5 all-gather.8
  354.6 34.7 all-gather.10
  401.0 180.9 all-gather.6

commit v2 on v1

--- a/solution.py
+++ b/solution.py
@@ -35,8 +35,35 @@
     return jax.vmap(lambda rows: apply_rotation(rows, sign))(value_rows)
 
 
-def gather(block):
-    return lax.all_gather(block, "fsdp", axis=0, tiled=True)
+def relay(block, tied=()):
+    n = lax.axis_size("fsdp")
+    me = lax.axis_index("fsdp")
+    up, down = [block], [block]
+    for hop in range(1, n):
+        if hop == n - 1:
+            last_up, last_down, tied = lax.optimization_barrier((up[-1], down[-1], tied))
+        else:
+            last_up, last_down = up[-1], down[-1]
+        up.append(lax.ppermute(last_up, "fsdp", [(f, f + 1) for f in range(hop - 1, n - 1)]))
+        down.append(lax.ppermute(last_down, "fsdp", [(f, f - 1) for f in range(1, n - hop + 1)]))
+    return [block] + [jnp.where(me >= j, up[j], down[n - j]) for j in range(1, n)], tied
+
+
+def gather(block, place, out, tied=()):
+    n = lax.axis_size("fsdp")
+    me = lax.axis_index("fsdp")
+    blocks, tied = relay(block, tied)
+    for j in range(n):
+        out = place(out, blocks[j], lax.rem(me + n - j, n))
+    return out, tied
+
+
+def place_rows(out, piece, f):
+    return lax.dynamic_update_slice_in_dim(out, piece, f * piece.shape[0], 0)
+
+
+def place_cols(out, piece, f):
+    return lax.dynamic_update_slice_in_dim(out, piece, f * piece.shape[1], 1)
 
 
 def attend(query_raw, key_raw, value_raw):
@@ -131,8 +158,15 @@
     model_cols = w_output.shape[2]
     total_rows = n * length
 
-    all_tokens = gather(tokens)
-    all_cotangent = gather(cotangent)
+    all_tokens, (later_cotangent, later_output) = gather(
+        tokens,
+        place_rows,
+        jnp.zeros((total_rows, width), jnp.bfloat16),
+        (cotangent, w_output),
+    )
+    all_cotangent, _ = gather(
+        later_cotangent, place_rows, jnp.zeros((total_rows, width), jnp.bfloat16)
+    )
 
     def pick_weight(d):
         return jnp.concatenate(
@@ -144,15 +178,9 @@
             axis=1,
         )
 
-    def place_rows(out, piece, f):
-        return lax.dynamic_update_slice_in_dim(out, piece, f * piece.shape[0], 0)
-
-    def place_cols(out, piece, f):
-        return lax.dynamic_update_slice_in_dim(out, piece, f * piece.shape[1], 1)
-
     w_in = exchange(pick_weight, place_rows, jnp.zeros((n * depth, own_cols), jnp.bfloat16))
     w_out_rows = exchange(
-        lambda d: lax.dynamic_slice_in_dim(w_output[0], d * own_query, own_query, 0),
+        lambda d: lax.dynamic_slice_in_dim(later_output[0], d * own_query, own_query, 0),
         place_cols,
         jnp.zeros((own_query, n * model_cols), jnp.bfloat16),
     )
@@ -164,7 +192,9 @@
     attn, saved = attend(query_raw, key_raw, value_raw)
 
     own_attn = attn.reshape(total_rows, own_query)
-    all_attn = lax.all_gather(own_attn, "fsdp", axis=1, tiled=True)
+    all_attn, _ = gather(
+        own_attn, place_cols, jnp.zeros((total_rows, n * own_query), jnp.bfloat16)
+    )
 
     d_attn = (
         lax.dot_general(

time: 650 us -> 572 us (0.88)
  waiting for transfers between devices: 417 us -> 287 us
  starting transfers between devices: 32.2 us -> 91.4 us
  local copies, waits for them, and re-layouts: 72.4 us -> 50.6 us
  other arithmetic: 37.9 us -> 51.3 us
    ppermute x0 -> x18, waiting for transfers between devices: none -> 139 us  [the longest x9 104 us: relay(): lax.ppermute(last_down, 'fsdp', [(f, f - 1) for f in range(1, n - hop + 1)])]
    ppermute x12, waiting for transfers between devices: 266 us -> 148 us  [exchange(): piece = lax.ppermute(pick(lax.rem(me + shift, n)), 'fsdp', pairs)]
    all_gather x3 -> x0, waiting for transfers between devices: 114 us -> none  [the longest x2 87.8 us: gather(): return lax.all_gather(block, 'fsdp', axis=0, tiled=True)]
    ppermute x0 -> x18, starting transfers between devices: none -> 64.3 us  [the longest x9 41.7 us: relay(): lax.ppermute(last_up, 'fsdp', [(f, f + 1) for f in range(hop - 1, n - 1)])]
    reduce_scatter x1, waiting for transfers between devices: 36 us -> 0.01 us  [outer_sync(): lax.psum_scatter(snapshot[0].astype(jnp.float32), 'replica', scatter_dime...]
    dynamic_update_slice x1 -> x7, other arithmetic: 1.41 us -> 16.2 us  [place_rows(): return lax.dynamic_update_slice_in_dim(out, piece, f * piece.shape[0], 0)]
    unnamed x70 -> x38, local copies, waits for them, and re-layouts: 13.5 us -> 4.69 us
    dynamic_update_slice x19 -> x17, local copies, waits for them, and re-layouts: 14.2 us -> 9.68 us  [place_cols(): return lax.dynamic_update_slice_in_dim(out, piece, f * piece.shape[1], 1)]
  transfers between devices with their start and end apart: 17 -> 32, of which waited for: 11 -> 14; matrix products, arithmetic and copies ran while one was open for 24% -> 29% of each run, Pallas kernels for 0% -> 0%
where the time goes in v2:
time: 572 us; the launch traced here: 561 us
  waiting for transfers between devices  287 us (50%)
  starting transfers between devices  91.4 us (16%)
  matrix products  65.9 us (12%)
  other arithmetic  51.3 us (9%)
  local copies, waits for them, and re-layouts  50.6 us (9%)
  between operations  15 us (3%)
    ppermute x12, waiting for transfers between devices, exchange(): piece = lax.ppermute(pick(lax.rem(me + shift, n)), 'fsdp', pairs)  148 us
    ppermute x9, waiting for transfers between devices, relay(): lax.ppermute(last_down, 'fsdp', [(f, f - 1) for f in range(1, n - hop + 1)])  104 us
    ppermute x9, starting transfers between devices, relay(): lax.ppermute(last_up, 'fsdp', [(f, f + 1) for f in range(hop - 1, n - 1)])  41.7 us
    ppermute x9, waiting for transfers between devices, relay(): lax.ppermute(last_up, 'fsdp', [(f, f + 1) for f in range(hop - 1, n - 1)])  34.9 us
    ppermute x12, starting transfers between devices, exchange(): piece = lax.ppermute(pick(lax.rem(me + shift, n)), 'fsdp', pairs)  27.1 us
    ppermute x9, starting transfers between devices, relay(): lax.ppermute(last_down, 'fsdp', [(f, f - 1) for f in range(1, n - hop + 1)])  22.6 us
    dynamic_update_slice x7, other arithmetic, place_rows(): return lax.dynamic_update_slice_in_dim(out, piece, f * piece.shape[0], 0)  16.2 us
  transfers between devices with their start and end apart: 32, of which 14 were waited for; matrix products, arithmetic and copies ran while one was open for 29% of the time, Pallas kernels for 0%

profile of v2, /device:TPU:0, one launch (start us, length us, event | category | flops | bytes accessed | tf_op | source)
XLA Modules:
  0.0 561.3 jit_solution(13246871537696954731)
XLA Ops:
  7.2 6.2 %collective-permute-start = (bf16[384,2048]{1,0:T(8,128)(2,1)}, bf16[384,2048]{1,0:T(8,128)(2,1)}, u32[]{:S(2)}, u32[]{:S(2)}) collective-permute-start(bf16[384,2048]{1,0:T(8,128)(2,1)} %param.9), channel_id=1, source_target_pairs={{0,1},{1,2},{2,3},{4,5},{5,6},{6,7},{8,9},{9,10},{10,11},{12,13},{... | collective-permute-start | bytes 4718600 | tf_op jit(solution)/shard_map/ppermute | solution.py:47
  14.8 31.5 %collective-permute-done = bf16[384,2048]{1,0:T(8,128)(2,1)} collective-permute-done((bf16[384,2048]{1,0:T(8,128)(2,1)}, bf16[384,2048]{1,0:T(8,128)(2,1)}, u32[]{:S(2)}, u32[]{:S(2)}) %collective-permute-start) | collective-permute-done | bytes 1572896 | tf_op jit(solution)/shard_map/ppermute | solution.py:47
  66.1 41.9 %collective-permute-done.3 = bf16[384,2048]{1,0:T(8,128)(2,1)} collective-permute-done((bf16[384,2048]{1,0:T(8,128)(2,1)}, bf16[384,2048]{1,0:T(8,128)(2,1)}, u32[]{:S(2)}, u32[]{:S(2)}) %collective-permute-start.3) | collective-permute-done | bytes 1572896 | tf_op jit(solution)/shard_map/ppermute | solution.py:48
  119.0 23.9 %collective-permute-done.7 = bf16[512,768]{1,0:T(8,128)(2,1)} collective-permute-done((bf16[512,768]{1,0:T(8,128)(2,1)}, bf16[512,768]{1,0:T(8,128)(2,1)}, u32[]{:S(2)}, u32[]{:S(2)}) %collective-permute-start.7) | collective-permute-done | bytes 786464 | tf_op jit(solution)/shard_map/ppermute | solution.py:119
  145.4 16.9 %collective-permute-start.18 = (bf16[384,2048]{1,0:T(8,128)(2,1)}, bf16[384,2048]{1,0:T(8,128)(2,1)}, u32[]{:S(2)}, u32[]{:S(2)}) collective-permute-start(bf16[384,2048]{1,0:T(8,128)(2,1)} %param.10), channel_id=1, source_target_pairs={{0,1},{1,2},{2,3},{4,5},{5,6},{6,7},{8,9},{9,10},{10,11},{12,13},{... | collective-permute-start | bytes 4718600 | tf_op jit(solution)/shard_map/ppermute | solution.py:47
  167.4 7.0 %collective-permute-done.4 = bf16[384,2048]{1,0:T(8,128)(2,1)} collective-permute-done((bf16[384,2048]{1,0:T(8,128)(2,1)}, bf16[384,2048]{1,0:T(8,128)(2,1)}, u32[]{:S(2)}, u32[]{:S(2)}) %collective-permute-start.4) | collective-permute-done | bytes 1572896 | tf_op jit(solution)/shard_map/ppermute | solution.py:48
  180.7 5.2 fusion.65
  198.1 20.3 %collective-permute-done.20 = bf16[384,2048]{1,0:T(8,128)(2,1)} collective-permute-done((bf16[384,2048]{1,0:T(8,128)(2,1)}, bf16[384,2048]{1,0:T(8,128)(2,1)}, u32[]{:S(2)}, u32[]{:S(2)}) %collective-permute-start.20) | collective-permute-done | bytes 1572896 | tf_op jit(solution)/shard_map/ppermute | solution.py:48
  218.4 12.3 %collective-permute-start.21 = (bf16[384,2048]{1,0:T(8,128)(2,1)}, bf16[384,2048]{1,0:T(8,128)(2,1)}, u32[]{:S(2)}, u32[]{:S(2)}) collective-permute-start(bf16[384,2048]{1,0:T(8,128)(2,1)} %collective-permute-done.20), channel_id=1, source_target_pairs={{1,0},{2,1},{5,4},{6,5},{9,8},{10,9},{13,12},{14,13},{17,16},{18,1... | collective-permute-start | bytes 4718600 | tf_op jit(solution)/shard_map/ppermute | solution.py:48
  236.2 10.0 %fusion.64 = (f32[4,4,384]{2,1,0:T(4,128)}, f32[4,4,384,384]{2,3,1,0:T(8,128)}) fusion(pred[384,384]{0,1:T(8,128)(4,1)} %iota_compare_fusion, bf16[4,384,1,64]{3,1,0,2:T(8,128)(2,1)} %get-tuple-element.49, bf16[4,384,1,64]{3,1,0,2:T(8,128)(2,1)} %get-tuple-element.48, bf16[4,384,4,64]{3,1,2,0:T(8,128)(2,1)S(1)} %get-tuple-element.27, ...), kind=kOutput, calls=%fused_computation.146 | convolution fusion | flops 617349504 | bytes 11575296 | tf_op jit(solution)/shard_map/sub | solution.py:82
  246.2 6.0 %fusion.27 = bf16[4,384,4,128]{1,3,2,0:T(8,128)(2,1)} fusion(bf16[4,384,128,1]{2,1,3,0:T(8,128)(2,1)} %bitcast.189, f32[4,4,384,384]{2,3,1,0:T(8,128)} %get-tuple-element.68, f32[4,4,384]{2,1,0:T(4,128)} %get-tuple-element.67), kind=kOutput, calls=%fused_computation.52 | convolution fusion | flops 609484800 | bytes 11427840 | tf_op jit(solution)/shard_map/sgqk,skd->sqgd/dot_general | solution.py:85
  256.3 9.6 %collective-permute-start.9 = (bf16[1536,512]{1,0:T(8,128)(2,1)}, bf16[1536,512]{1,0:T(8,128)(2,1)}, u32[]{:S(2)}, u32[]{:S(2)}) collective-permute-start(bf16[1536,512]{1,0:T(8,128)(2,1)} %bitcast.181), channel_id=1, source_target_pairs={{0,1},{1,2},{2,3},{4,5},{5,6},{6,7},{8,9},{9,10},{10,11},{12,13},{... | collective-permute-start | bytes 4718600 | tf_op jit(solution)/shard_map/ppermute | solution.py:47
  286.2 40.1 %collective-permute-done.25 = bf16[512,512]{1,0:T(8,128)(2,1)} collective-permute-done((bf16[512,512]{1,0:T(8,128)(2,1)}, bf16[512,512]{1,0:T(8,128)(2,1)}, u32[]{:S(2)}, u32[]{:S(2)}) %collective-permute-start.25) | collective-permute-done | bytes 524320 | tf_op jit(solution)/shard_map/ppermute | solution.py:119
  329.9 25.3 %collective-permute-done.26 = bf16[512,512]{1,0:T(8,128)(2,1)S(1)} collective-permute-done((bf16[512,512]{1,0:T(8,128)(2,1)}, bf16[512,512]{1,0:T(8,128)(2,1)S(1)}, u32[]{:S(2)}, u32[]{:S(2)}) %collective-permute-start.26) | collective-permute-done | bytes 524320 | tf_op jit(solution)/shard_map/ppermute | solution.py:119
  371.5 8.0 %convolution_convert_fusion.2 = bf16[1536,512]{1,0:T(8,128)(2,1)} fusion(bf16[1536,2048]{1,0:T(8,128)(2,1)} %select_dynamic-update-slice_fusion, bf16[512,2048]{1,0:T(8,128)(2,1)} %constant_dynamic-update-slice_fusion), kind=kOutput, calls=%fused_computation.22 | convolution fusion | flops 3222011904 | bytes 9961472 | tf_op jit(solution)/shard_map/dot_general | solution.py:200
  383.4 10.0 %fusion.1 = (f32[4,4,384]{2,1,0:T(4,128)}, f32[4,384,384,4]{2,1,3,0:T(8,128)}) fusion(f32[4,4,384,384]{2,3,1,0:T(8,128)} %get-tuple-element.68, f32[4,4,384]{2,1,0:T(4,128)} %get-tuple-element.67, bf16[4,384,128,1]{2,1,3,0:T(8,128)(2,1)} %bitcast.190, bf16[4,384,4,128]{3,2,1,0:T(4,128)(2,1)} %reshape.151), kind=kOutput, calls=%fused_computation.3 | convolution fusion | flops 611051520 | bytes 20889600 | tf_op jit(solution)/shard_map/sqgd,skd->sgqk/dot_general | solution.py:93
  393.5 9.9 %fusion.3 = bf16[4,4,384,384]{2,3,1,0:T(8,128)(2,1)} fusion(f32[4,384,384,4]{2,1,3,0:T(8,128)} %get-tuple-element.70, f32[4,4,384]{2,1,0:T(4,128)} %get-tuple-element.69, f32[4,4,384,384]{2,3,1,0:T(8,128)} %get-tuple-element.68, f32[4,4,384]{2,1,0:T(4,128)} %get-tuple-element.67), kind=kLoop, calls=%fused_computation.5 | loop fusion | flops 9437184 | bytes 23642112 | tf_op jit(solution)/shard_map/convert_element_type | solution.py:94
  409.6 5.1 fusion.40
  418.9 5.7 %convolution_convert_fusion = bf16[2048,768]{1,0:T(8,128)(2,1)S(1)} fusion(bf16[1536,2048]{1,0:T(8,128)(2,1)S(1)} %bitcast.186, bf16[1536,128]{1,0:T(8,128)(2,1)S(1)} %bitcast.192, bf16[1536,128]{1,0:T(8,128)(2,1)S(1)} %bitcast.191, bf16[1536,512]{1,0:T(8,128)(2,1)S(1)} %bitcast.188), kind=kOutput, calls=%fused_computation.14 | convolution fusion | flops 4840488960 | bytes 11796480 | tf_op jit(solution)/shard_map/dot_general | solution.py:210
  435.1 12.1 %collective-permute-done.27 = bf16[512,768]{1,0:T(8,128)(2,1)S(1)} collective-permute-done((bf16[512,768]{1,0:T(8,128)(2,1)S(1)}, bf16[512,768]{1,0:T(8,128)(2,1)S(1)}, u32[]{:S(2)}, u32[]{:S(2)}) %collective-permute-start.27) | collective-permute-done | bytes 786464 | tf_op jit(solution)/shard_map/ppermute | solution.py:119
  447.3 27.4 %collective-permute-done.28 = bf16[512,768]{1,0:T(8,128)(2,1)S(1)} collective-permute-done((bf16[512,768]{1,0:T(8,128)(2,1)S(1)}, bf16[512,768]{1,0:T(8,128)(2,1)S(1)}, u32[]{:S(2)}, u32[]{:S(2)}) %collective-permute-start.28) | collective-permute-done | bytes 786464 | tf_op jit(solution)/shard_map/ppermute | solution.py:119
  476.5 31.7 %collective-permute-done.13 = bf16[1536,512]{1,0:T(8,128)(2,1)S(1)} collective-permute-done((bf16[1536,512]{1,0:T(8,128)(2,1)}, bf16[1536,512]{1,0:T(8,128)(2,1)S(1)}, u32[]{:S(2)}, u32[]{:S(2)}) %collective-permute-start.13) | collective-permute-done | bytes 1572896 | tf_op jit(solution)/shard_map/ppermute | solution.py:48
  522.5 6.0 %fusion.8 = bf16[1,2048,512]{2,1,0:T(8,128)(2,1)} fusion(bf16[1536,2048]{1,0:T(8,128)(2,1)S(1)} %select_dynamic-update-slice_fusion.3, bf16[1536,2048]{1,0:T(8,128)(2,1)} %select_dynamic-update-slice_fusion, s32[]{:T(128)S(6)} %select_n.156), kind=kOutput, calls=%fused_computation.23 | convolution fusion | flops 3222274048 | bytes 9961476 | tf_op jit(solution)/shard_map/dot_general | solution.py:242
  533.4 15.1 %collective-permute-done.16 = bf16[384,512]{1,0:T(8,128)(2,1)S(1)} collective-permute-done((bf16[384,512]{1,0:T(8,128)(2,1)S(1)}, bf16[384,512]{1,0:T(8,128)(2,1)S(1)}, u32[]{:S(2)}, u32[]{:S(2)}) %collective-permute-start.16) | collective-permute-done | bytes 393248 | tf_op jit(solution)/shard_map/ppermute | solution.py:119
  (163 shorter events, 159.0 us)
Async XLA Ops:
  7.2 348.8 %reduce-scatter.2.cloned.1.call-start = ((), (), s32[]{:S(2)}) async-start(), calls=%async_computation.1 | async-start | bytes 4718592 | tf_op jit(solution)/shard_map/reduce_scatter | solution.py:125
  51.5 56.4 %collective-permute-start.3 = (bf16[384,2048]{1,0:T(8,128)(2,1)}, bf16[384,2048]{1,0:T(8,128)(2,1)}, u32[]{:S(2)}, u32[]{:S(2)}) collective-permute-start(bf16[384,2048]{1,0:T(8,128)(2,1)} %collective-permute-done.2), channel_id=1, source_target_pairs={{1,0},{2,1},{5,4},{6,5},{9,8},{10,9},{13,12},{14,13},{17,16},{18,1... | collective-permute-start | bytes 4718600 | tf_op jit(solution)/shard_map/ppermute | solution.py:48
  56.3 61.5 %collective-permute-start.6 = (bf16[512,768]{1,0:T(8,128)(2,1)}, bf16[512,768]{1,0:T(8,128)(2,1)}, u32[]{:S(2)}, u32[]{:S(2)}) collective-permute-start(bf16[512,768]{1,0:T(8,128)(2,1)} %pad_maximum_fusion.2), channel_id=1, source_target_pairs={{0,1},{1,2},{2,3},{3,0},{4,5},{5,6},{6,7},{7,4},{8,9},{9,10},{10,1... | collective-permute-start | bytes 2359304 | tf_op jit(solution)/shard_map/ppermute | solution.py:119
  59.9 83.1 %collective-permute-start.7 = (bf16[512,768]{1,0:T(8,128)(2,1)}, bf16[512,768]{1,0:T(8,128)(2,1)}, u32[]{:S(2)}, u32[]{:S(2)}) collective-permute-start(bf16[512,768]{1,0:T(8,128)(2,1)} %pad_maximum_fusion.3), channel_id=1, source_target_pairs={{0,2},{1,3},{2,0},{3,1},{4,6},{5,7},{6,4},{7,5},{8,10},{9,11},{10,... | collective-permute-start | bytes 2359304 | tf_op jit(solution)/shard_map/ppermute | solution.py:119
  63.1 81.0 %collective-permute-start.8 = (bf16[512,768]{1,0:T(8,128)(2,1)}, bf16[512,768]{1,0:T(8,128)(2,1)}, u32[]{:S(2)}, u32[]{:S(2)}) collective-permute-start(bf16[512,768]{1,0:T(8,128)(2,1)} %pad_maximum_fusion.4), channel_id=1, source_target_pairs={{0,3},{1,0},{2,1},{3,2},{4,7},{5,4},{6,5},{7,6},{8,11},{9,8},{10,9... | collective-permute-start | bytes 2359304 | tf_op jit(solution)/shard_map/ppermute | solution.py:119
  107.9 66.5 %collective-permute-start.4 = (bf16[384,2048]{1,0:T(8,128)(2,1)}, bf16[384,2048]{1,0:T(8,128)(2,1)}, u32[]{:S(2)}, u32[]{:S(2)}) collective-permute-start(bf16[384,2048]{1,0:T(8,128)(2,1)} %collective-permute-done.3), channel_id=1, source_target_pairs={{1,0},{5,4},{9,8},{13,12},{17,16},{21,20},{25,24},{29,28}} | collective-permute-start | bytes 4718600 | tf_op jit(solution)/shard_map/ppermute | solution.py:48
  111.9 438.2 %all-gather.2.cloned.1.call-start = ((), (), s32[]{:S(2)}) async-start(), calls=%async_computation.2 | async-start | bytes 4718592 | tf_op jit(solution)/shard_map/all_gather | solution.py:132
  116.9 61.7 %collective-permute-start.5 = (bf16[384,2048]{1,0:T(8,128)(2,1)}, bf16[384,2048]{1,0:T(8,128)(2,1)S(1)}, u32[]{:S(2)}, u32[]{:S(2)}) collective-permute-start(bf16[384,2048]{1,0:T(8,128)(2,1)} %collective-permute-done.1), channel_id=1, source_target_pairs={{2,3},{6,7},{10,11},{14,15},{18,19},{22,23},{26,27},{30,31}} | collective-permute-start | bytes 4718600 | tf_op jit(solution)/shard_map/ppermute | solution.py:47
  145.4 50.9 %collective-permute-start.18 = (bf16[384,2048]{1,0:T(8,128)(2,1)}, bf16[384,2048]{1,0:T(8,128)(2,1)}, u32[]{:S(2)}, u32[]{:S(2)}) collective-permute-start(bf16[384,2048]{1,0:T(8,128)(2,1)} %param.10), channel_id=1, source_target_pairs={{0,1},{1,2},{2,3},{4,5},{5,6},{6,7},{8,9},{9,10},{10,11},{12,13},{... | collective-permute-start | bytes 4718600 | tf_op jit(solution)/shard_map/ppermute | solution.py:47
  162.3 56.1 %collective-permute-start.20 = (bf16[384,2048]{1,0:T(8,128)(2,1)}, bf16[384,2048]{1,0:T(8,128)(2,1)}, u32[]{:S(2)}, u32[]{:S(2)}) collective-permute-start(bf16[384,2048]{1,0:T(8,128)(2,1)} %param.10), channel_id=1, source_target_pairs={{1,0},{2,1},{3,2},{5,4},{6,5},{7,6},{9,8},{10,9},{11,10},{13,12},{... | collective-permute-start | bytes 4718600 | tf_op jit(solution)/shard_map/ppermute | solution.py:48
  164.7 108.3 %collective-permute-start.24 = (bf16[512,512]{1,0:T(8,128)(2,1)}, bf16[512,512]{1,0:T(8,128)(2,1)}, u32[]{:S(2)}, u32[]{:S(2)}) collective-permute-start(bf16[512,512]{1,0:T(8,128)(2,1)} %get-tuple-element.37), channel_id=1, source_target_pairs={{0,1},{1,2},{2,3},{3,0},{4,5},{5,6},{6,7},{7,4},{8,9},{9,10},{10,1... | collective-permute-start | bytes 1572872 | tf_op jit(solution)/shard_map/ppermute | solution.py:119
  196.2 70.9 %collective-permute-start.19 = (bf16[384,2048]{1,0:T(8,128)(2,1)}, bf16[384,2048]{1,0:T(8,128)(2,1)}, u32[]{:S(2)}, u32[]{:S(2)}) collective-permute-start(bf16[384,2048]{1,0:T(8,128)(2,1)} %collective-permute-done.18), channel_id=1, source_target_pairs={{1,2},{2,3},{5,6},{6,7},{9,10},{10,11},{13,14},{14,15},{17,18},{18... | collective-permute-start | bytes 4718600 | tf_op jit(solution)/shard_map/ppermute | solution.py:47
  218.4 48.8 %collective-permute-start.21 = (bf16[384,2048]{1,0:T(8,128)(2,1)}, bf16[384,2048]{1,0:T(8,128)(2,1)}, u32[]{:S(2)}, u32[]{:S(2)}) collective-permute-start(bf16[384,2048]{1,0:T(8,128)(2,1)} %collective-permute-done.20), channel_id=1, source_target_pairs={{1,0},{2,1},{5,4},{6,5},{9,8},{10,9},{13,12},{14,13},{17,16},{18,1... | collective-permute-start | bytes 4718600 | tf_op jit(solution)/shard_map/ppermute | solution.py:48
  256.3 102.3 %collective-permute-start.9 = (bf16[1536,512]{1,0:T(8,128)(2,1)}, bf16[1536,512]{1,0:T(8,128)(2,1)}, u32[]{:S(2)}, u32[]{:S(2)}) collective-permute-start(bf16[1536,512]{1,0:T(8,128)(2,1)} %bitcast.181), channel_id=1, source_target_pairs={{0,1},{1,2},{2,3},{4,5},{5,6},{6,7},{8,9},{9,10},{10,11},{12,13},{... | collective-permute-start | bytes 4718600 | tf_op jit(solution)/shard_map/ppermute | solution.py:47
  265.9 94.5 %collective-permute-start.11 = (bf16[1536,512]{1,0:T(8,128)(2,1)}, bf16[1536,512]{1,0:T(8,128)(2,1)}, u32[]{:S(2)}, u32[]{:S(2)}) collective-permute-start(bf16[1536,512]{1,0:T(8,128)(2,1)} %bitcast.181), channel_id=1, source_target_pairs={{1,0},{2,1},{3,2},{5,4},{6,5},{7,6},{9,8},{10,9},{11,10},{13,12},{... | collective-permute-start | bytes 4718600 | tf_op jit(solution)/shard_map/ppermute | solution.py:48
  267.2 94.5 %collective-permute-start.22 = (bf16[384,2048]{1,0:T(8,128)(2,1)}, bf16[384,2048]{1,0:T(8,128)(2,1)}, u32[]{:S(2)}, u32[]{:S(2)}) collective-permute-start(bf16[384,2048]{1,0:T(8,128)(2,1)} %collective-permute-done.21), channel_id=1, source_target_pairs={{1,0},{5,4},{9,8},{13,12},{17,16},{21,20},{25,24},{29,28}} | collective-permute-start | bytes 4718600 | tf_op jit(solution)/shard_map/ppermute | solution.py:48
  268.5 57.8 %collective-permute-start.25 = (bf16[512,512]{1,0:T(8,128)(2,1)}, bf16[512,512]{1,0:T(8,128)(2,1)}, u32[]{:S(2)}, u32[]{:S(2)}) collective-permute-start(bf16[512,512]{1,0:T(8,128)(2,1)} %get-tuple-element.36), channel_id=1, source_target_pairs={{0,2},{1,3},{2,0},{3,1},{4,6},{5,7},{6,4},{7,5},{8,10},{9,11},{10,... | collective-permute-start | bytes 1572872 | tf_op jit(solution)/shard_map/ppermute | solution.py:119
  273.1 82.1 %collective-permute-start.26 = (bf16[512,512]{1,0:T(8,128)(2,1)}, bf16[512,512]{1,0:T(8,128)(2,1)S(1)}, u32[]{:S(2)}, u32[]{:S(2)}) collective-permute-start(bf16[512,512]{1,0:T(8,128)(2,1)} %get-tuple-element.35), channel_id=1, source_target_pairs={{0,3},{1,0},{2,1},{3,2},{4,7},{5,4},{6,5},{7,6},{8,11},{9,8},{10,9... | collective-permute-start | bytes 1572872 | tf_op jit(solution)/shard_map/ppermute | solution.py:119
  358.6 74.0 %collective-permute-start.10 = (bf16[1536,512]{1,0:T(8,128)(2,1)}, bf16[1536,512]{1,0:T(8,128)(2,1)}, u32[]{:S(2)}, u32[]{:S(2)}) collective-permute-start(bf16[1536,512]{1,0:T(8,128)(2,1)} %collective-permute-done.9), channel_id=1, source_target_pairs={{1,2},{2,3},{5,6},{6,7},{9,10},{10,11},{13,14},{14,15},{17,18},{18... | collective-permute-start | bytes 4718600 | tf_op jit(solution)/shard_map/ppermute | solution.py:47
  360.4 72.2 %collective-permute-start.12 = (bf16[1536,512]{1,0:T(8,128)(2,1)}, bf16[1536,512]{1,0:T(8,128)(2,1)}, u32[]{:S(2)}, u32[]{:S(2)}) collective-permute-start(bf16[1536,512]{1,0:T(8,128)(2,1)} %collective-permute-done.11), channel_id=1, source_target_pairs={{1,0},{2,1},{5,4},{6,5},{9,8},{10,9},{13,12},{14,13},{17,16},{18,1... | collective-permute-start | bytes 4718600 | tf_op jit(solution)/shard_map/ppermute | solution.py:48
  427.6 47.1 %collective-permute-start.28 = (bf16[512,768]{1,0:T(8,128)(2,1)S(1)}, bf16[512,768]{1,0:T(8,128)(2,1)S(1)}, u32[]{:S(2)}, u32[]{:S(2)}) collective-permute-start(bf16[512,768]{1,0:T(8,128)(2,1)S(1)} %get-tuple-element.31), channel_id=1, source_target_pairs={{0,2},{1,3},{2,0},{3,1},{4,6},{5,7},{6,4},{7,5},{8,10},{9,11},{10,... | collective-permute-start | bytes 2359304 | tf_op jit(solution)/shard_map/ppermute | solution.py:119
  429.7 45.2 %collective-permute-start.29 = (bf16[512,768]{1,0:T(8,128)(2,1)S(1)}, bf16[512,768]{1,0:T(8,128)(2,1)S(1)}, u32[]{:S(2)}, u32[]{:S(2)}) collective-permute-start(bf16[512,768]{1,0:T(8,128)(2,1)S(1)} %get-tuple-element.30), channel_id=1, source_target_pairs={{0,3},{1,0},{2,1},{3,2},{4,7},{5,4},{6,5},{7,6},{8,11},{9,8},{10,9... | collective-permute-start | bytes 2359304 | tf_op jit(solution)/shard_map/ppermute | solution.py:119
  432.6 75.6 %collective-permute-start.13 = (bf16[1536,512]{1,0:T(8,128)(2,1)}, bf16[1536,512]{1,0:T(8,128)(2,1)S(1)}, u32[]{:S(2)}, u32[]{:S(2)}) collective-permute-start(bf16[1536,512]{1,0:T(8,128)(2,1)} %collective-permute-done.12), channel_id=1, source_target_pairs={{1,0},{5,4},{9,8},{13,12},{17,16},{21,20},{25,24},{29,28}} | collective-permute-start | bytes 4718600 | tf_op jit(solution)/shard_map/ppermute | solution.py:48
  433.9 76.9 %collective-permute-start.14 = (bf16[1536,512]{1,0:T(8,128)(2,1)}, bf16[1536,512]{1,0:T(8,128)(2,1)S(1)}, u32[]{:S(2)}, u32[]{:S(2)}) collective-permute-start(bf16[1536,512]{1,0:T(8,128)(2,1)} %collective-permute-done.10), channel_id=1, source_target_pairs={{2,3},{6,7},{10,11},{14,15},{18,19},{22,23},{26,27},{30,31}} | collective-permute-start | bytes 4718600 | tf_op jit(solution)/shard_map/ppermute | solution.py:47
  (26 other events, 489.5 us)
Sparse Core Ops, SparseCore 0:
  112.0 68.7 reduce-scatter.1
  358.7 34.9 all-gather.1

commit v3 on v2

--- a/solution.py
+++ b/solution.py
@@ -86,14 +86,18 @@
     return attn.astype(jnp.bfloat16), (query_rows, key_rows, value_rows, probs, probs_b)
 
 
-def attend_gradient(saved, d_attn):
-    query_rows, key_rows, value_rows, probs, probs_b = saved
+def score_gradient(saved, d_attn):
+    _, _, value_rows, probs, _ = saved
+    d_probs = jnp.einsum("sqgd,skd->sgqk", d_attn, value_rows, preferred_element_type=jnp.float32)
+    return (probs * (d_probs - jnp.sum(d_probs * probs, axis=-1, keepdims=True))).astype(
+        jnp.bfloat16
+    )
+
+
+def attend_gradient(saved, d_attn, d_scores):
+    query_rows, key_rows, _, _, probs_b = saved
     scale = HEAD_SIZE ** (-0.5)
     d_values = jnp.einsum("sgqk,sqgd->skd", probs_b, d_attn, preferred_element_type=jnp.float32)
-    d_probs = jnp.einsum("sqgd,skd->sgqk", d_attn, value_rows, preferred_element_type=jnp.float32)
-    d_scores = (probs * (d_probs - jnp.sum(d_probs * probs, axis=-1, keepdims=True))).astype(
-        jnp.bfloat16
-    )
     d_queries = (
         jnp.einsum("sgqk,skd->sqgd", d_scores, key_rows, preferred_element_type=jnp.float32) * scale
     )
@@ -110,15 +114,28 @@
     )
 
 
-def exchange(pick, place, out):
+def send(pick):
+    n = lax.axis_size("fsdp")
+    me = lax.axis_index("fsdp")
+    return [
+        lax.ppermute(
+            pick(lax.rem(me + shift, n)), "fsdp", [(f, (f + shift) % n) for f in range(n)]
+        )
+        for shift in range(1, n)
+    ]
+
+
+def place_pieces(pick, pieces, place, out):
     n = lax.axis_size("fsdp")
     me = lax.axis_index("fsdp")
     out = place(out, pick(me), me)
-    for shift in range(1, n):
-        pairs = [(f, (f + shift) % n) for f in range(n)]
-        piece = lax.ppermute(pick(lax.rem(me + shift, n)), "fsdp", pairs)
+    for shift, piece in enumerate(pieces, 1):
         out = place(out, piece, lax.rem(me + n - shift, n))
     return out
+
+
+def exchange(pick, place, out):
+    return place_pieces(pick, send(pick), place, out)
 
 
 def outer_sync(snapshot, global_output, momentum, w_output):
@@ -192,10 +209,6 @@
     attn, saved = attend(query_raw, key_raw, value_raw)
 
     own_attn = attn.reshape(total_rows, own_query)
-    all_attn, _ = gather(
-        own_attn, place_cols, jnp.zeros((total_rows, n * own_query), jnp.bfloat16)
-    )
-
     d_attn = (
         lax.dot_general(
             all_cotangent,
@@ -206,7 +219,13 @@
         .astype(jnp.bfloat16)
         .reshape(n, length, group, HEAD_SIZE)
     )
-    d_in = attend_gradient(saved, d_attn)
+    all_attn, d_scores = gather(
+        own_attn,
+        place_cols,
+        jnp.zeros((total_rows, n * own_query), jnp.bfloat16),
+        score_gradient(saved, d_attn),
+    )
+    d_in = attend_gradient(saved, d_attn, d_scores)
     grad_in = lax.dot_general(
         all_tokens, d_in, (((0,), (0,)), ((), ())), preferred_element_type=jnp.float32
     ).astype(jnp.bfloat16)
@@ -219,25 +238,29 @@
             place_cols(grad_value, piece[:, own_query + own_key :], f),
         )
 
-    grad_query, grad_key, grad_value = exchange(
-        lambda d: lax.dynamic_slice_in_dim(grad_in, d * depth, depth, 0),
+    def pick_grads(d):
+        return lax.dynamic_slice_in_dim(grad_in, d * depth, depth, 0)
+
+    grad_pieces = send(pick_grads)
+    own_token_cols = lax.dynamic_slice_in_dim(all_tokens, me * model_cols, model_cols, 1)
+    out_cols = (
+        own_token_cols.astype(jnp.float32)
+        + jnp.dot(all_attn, w_output[0], preferred_element_type=jnp.float32)
+    ).astype(jnp.bfloat16)
+    def pick_out(d):
+        return lax.dynamic_slice_in_dim(out_cols, d * length, length, 0)
+
+    out_pieces = send(pick_out)
+    grad_pieces, _ = lax.optimization_barrier((grad_pieces, out_cols))
+    grad_query, grad_key, grad_value = place_pieces(
+        pick_grads,
+        grad_pieces,
         place_grads,
         tuple(
             jnp.zeros(w.shape[1:], jnp.bfloat16)
             for w in (w_query, replica_key_weight, replica_value_weight)
         ),
     )
-
-    own_token_cols = lax.dynamic_slice_in_dim(all_tokens, me * model_cols, model_cols, 1)
-    out_cols = (
-        own_token_cols.astype(jnp.float32)
-        + jnp.dot(all_attn, w_output[0], preferred_element_type=jnp.float32)
-    ).astype(jnp.bfloat16)
-    block_out = exchange(
-        lambda d: lax.dynamic_slice_in_dim(out_cols, d * length, length, 0),
-        place_cols,
-        jnp.zeros((length, width), jnp.bfloat16),
-    )
     own_cotangent_cols = lax.dynamic_slice_in_dim(all_cotangent, me * model_cols, model_cols, 1)
     grad_output = lax.dot_general(
         all_attn, own_cotangent_cols, (((0,), (0,)), ((), ())), preferred_element_type=jnp.float32
@@ -245,6 +268,10 @@
 
     merged_output, global_new, momentum_new = outer_sync(
         snapshot, global_output, momentum, w_output
+    )
+    out_pieces[0], merged_output = lax.optimization_barrier((out_pieces[0], merged_output))
+    block_out = place_pieces(
+        pick_out, out_pieces, place_cols, jnp.zeros((length, width), jnp.bfloat16)
     )
     return (
         block_out,

time: 572 us -> 530 us (0.927)
  waiting for transfers between devices: 287 us -> 233 us
  starting transfers between devices: 91.4 us -> 112 us
  matrix products: 65.9 us -> 58.1 us
    ppermute x12, waiting for transfers between devices: 148 us -> 24.1 us  [send(): lax.ppermute(pick(lax.rem(me + shift, n)), 'fsdp', [(f, (f + shift) % n)...]
    ppermute x9, waiting for transfers between devices: 104 us -> 172 us  [relay(): lax.ppermute(last_down, 'fsdp', [(f, f - 1) for f in range(1, n - hop + 1)])]
    ppermute x9, starting transfers between devices: 41.7 us -> 60.2 us  [relay(): lax.ppermute(last_up, 'fsdp', [(f, f + 1) for f in range(hop - 1, n - 1)])]
    sub x0 -> x1, other arithmetic: none -> 11.5 us  [score_gradient(): d_probs - jnp.sum(d_probs * probs, axis=-1, keepdims=True)]
    convert_element_type x1 -> x0, other arithmetic: 9.91 us -> none  [attend_gradient(): (probs * (d_probs - jnp.sum(d_probs * probs, axis=-1, keepdims=True))).as...]
    dot_general x1, matrix products: 10 us -> 2.94 us  [score_gradient(): jnp.einsum('sqgd,skd->sgqk', d_attn, value_rows, preferred_element_type=j...]
  transfers between devices with their start and end apart: 32 -> 32, of which waited for: 14 -> 10; matrix products, arithmetic and copies ran while one was open for 29% -> 30% of each run, Pallas kernels for 0% -> 0%
where the time goes in v3:
time: 530 us; the launch traced here: 524 us
  waiting for transfers between devices  233 us (44%)
  starting transfers between devices  112 us (21%)
  matrix products  58.1 us (11%)
  other arithmetic  54.8 us (10%)
  local copies, waits for them, and re-layouts  50.3 us (9%)
  between operations  15.3 us (3%)
    ppermute x9, waiting for transfers between devices, relay(): lax.ppermute(last_down, 'fsdp', [(f, f - 1) for f in range(1, n - hop + 1)])  172 us
    ppermute x9, starting transfers between devices, relay(): lax.ppermute(last_up, 'fsdp', [(f, f + 1) for f in range(hop - 1, n - 1)])  60.2 us
    ppermute x9, waiting for transfers between devices, relay(): lax.ppermute(last_up, 'fsdp', [(f, f + 1) for f in range(hop - 1, n - 1)])  36.1 us
    ppermute x12, starting transfers between devices, send(): lax.ppermute(pick(lax.rem(me + shift, n)), 'fsdp', [(f, (f + shift) % n)...  30.2 us
    ppermute x12, waiting for transfers between devices, send(): lax.ppermute(pick(lax.rem(me + shift, n)), 'fsdp', [(f, (f + shift) % n)...  24.1 us
    ppermute x9, starting transfers between devices, relay(): lax.ppermute(last_down, 'fsdp', [(f, f - 1) for f in range(1, n - hop + 1)])  21.8 us
    dynamic_update_slice x7, other arithmetic, place_rows(): return lax.dynamic_update_slice_in_dim(out, piece, f * piece.shape[0], 0)  14.8 us
    dynamic_update_slice x17, local copies, waits for them, and re-layouts, place_cols(): return lax.dynamic_update_slice_in_dim(out, piece, f * piece.shape[1], 1)  13.5 us
  transfers between devices with their start and end apart: 32, of which 10 were waited for; matrix products, arithmetic and copies ran while one was open for 30% of the time, Pallas kernels for 0%

profile of v3, /device:TPU:0, one launch (start us, length us, event | category | flops | bytes accessed | tf_op | source)
XLA Modules:
  0.0 523.5 jit_solution(13473392422821270458)
XLA Ops:
  7.2 6.2 %collective-permute-start = (bf16[384,2048]{1,0:T(8,128)(2,1)}, bf16[384,2048]{1,0:T(8,128)(2,1)}, u32[]{:S(2)}, u32[]{:S(2)}) collective-permute-start(bf16[384,2048]{1,0:T(8,128)(2,1)} %param.9), channel_id=1, source_target_pairs={{0,1},{1,2},{2,3},{4,5},{5,6},{6,7},{8,9},{9,10},{10,11},{12,13},{... | collective-permute-start | bytes 4718600 | tf_op jit(solution)/shard_map/ppermute | solution.py:47
  14.7 31.5 %collective-permute-done = bf16[384,2048]{1,0:T(8,128)(2,1)} collective-permute-done((bf16[384,2048]{1,0:T(8,128)(2,1)}, bf16[384,2048]{1,0:T(8,128)(2,1)}, u32[]{:S(2)}, u32[]{:S(2)}) %collective-permute-start) | collective-permute-done | bytes 1572896 | tf_op jit(solution)/shard_map/ppermute | solution.py:47
  66.1 41.7 %collective-permute-done.3 = bf16[384,2048]{1,0:T(8,128)(2,1)} collective-permute-done((bf16[384,2048]{1,0:T(8,128)(2,1)}, bf16[384,2048]{1,0:T(8,128)(2,1)}, u32[]{:S(2)}, u32[]{:S(2)}) %collective-permute-start.3) | collective-permute-done | bytes 1572896 | tf_op jit(solution)/shard_map/ppermute | solution.py:48
  118.9 24.1 %collective-permute-done.7 = bf16[512,768]{1,0:T(8,128)(2,1)} collective-permute-done((bf16[512,768]{1,0:T(8,128)(2,1)}, bf16[512,768]{1,0:T(8,128)(2,1)}, u32[]{:S(2)}, u32[]{:S(2)}) %collective-permute-start.7) | collective-permute-done | bytes 786464 | tf_op jit(solution)/shard_map/ppermute | solution.py:121
  145.4 16.9 %collective-permute-start.13 = (bf16[384,2048]{1,0:T(8,128)(2,1)}, bf16[384,2048]{1,0:T(8,128)(2,1)}, u32[]{:S(2)}, u32[]{:S(2)}) collective-permute-start(bf16[384,2048]{1,0:T(8,128)(2,1)} %param.10), channel_id=1, source_target_pairs={{0,1},{1,2},{2,3},{4,5},{5,6},{6,7},{8,9},{9,10},{10,11},{12,13},{... | collective-permute-start | bytes 4718600 | tf_op jit(solution)/shard_map/ppermute | solution.py:47
  167.4 7.0 %collective-permute-done.4 = bf16[384,2048]{1,0:T(8,128)(2,1)} collective-permute-done((bf16[384,2048]{1,0:T(8,128)(2,1)}, bf16[384,2048]{1,0:T(8,128)(2,1)}, u32[]{:S(2)}, u32[]{:S(2)}) %collective-permute-start.4) | collective-permute-done | bytes 1572896 | tf_op jit(solution)/shard_map/ppermute | solution.py:48
  178.6 10.2 %collective-permute-start.21 = (bf16[512,512]{1,0:T(8,128)(2,1)}, bf16[512,512]{1,0:T(8,128)(2,1)}, u32[]{:S(2)}, u32[]{:S(2)}) collective-permute-start(bf16[512,512]{1,0:T(8,128)(2,1)} %get-tuple-element.47), channel_id=1, source_target_pairs={{0,3},{1,0},{2,1},{3,2},{4,7},{5,4},{6,5},{7,6},{8,11},{9,8},{10,9... | collective-permute-start | bytes 1572872 | tf_op jit(solution)/shard_map/ppermute | solution.py:121
  191.0 5.2 fusion.57
  205.0 17.7 %collective-permute-done.15 = bf16[384,2048]{1,0:T(8,128)(2,1)} collective-permute-done((bf16[384,2048]{1,0:T(8,128)(2,1)}, bf16[384,2048]{1,0:T(8,128)(2,1)}, u32[]{:S(2)}, u32[]{:S(2)}) %collective-permute-start.15) | collective-permute-done | bytes 1572896 | tf_op jit(solution)/shard_map/ppermute | solution.py:48
  229.8 10.0 %fusion.56 = (f32[4,4,384]{2,1,0:T(4,128)}, f32[4,4,384,384]{2,3,1,0:T(8,128)}) fusion(pred[384,384]{0,1:T(8,128)(4,1)} %iota_compare_fusion, bf16[4,384,1,64]{3,1,0,2:T(8,128)(2,1)} %get-tuple-element.61, bf16[4,384,1,64]{3,1,0,2:T(8,128)(2,1)} %get-tuple-element.60, bf16[4,384,4,64]{3,1,2,0:T(8,128)(2,1)S(1)} %get-tuple-element.39, ...), kind=kOutput, calls=%fused_computation.138 | convolution fusion | flops 617349504 | bytes 11575296 | tf_op jit(solution)/shard_map/sub | solution.py:82
  239.8 4.8 fusion.28
  247.3 27.8 %collective-permute-start.9 = (bf16[1536,512]{1,0:T(8,128)(2,1)}, bf16[1536,512]{1,0:T(8,128)(2,1)}, u32[]{:S(2)}, u32[]{:S(2)}) collective-permute-start(bf16[1536,512]{1,0:T(8,128)(2,1)} %bitcast.166), channel_id=1, source_target_pairs={{0,1},{1,2},{2,3},{4,5},{5,6},{6,7},{8,9},{9,10},{10,11},{12,13},{... | collective-permute-start | bytes 4718600 | tf_op jit(solution)/shard_map/ppermute | solution.py:47
  294.9 4.5 collective-permute-done.9
  301.3 23.0 %collective-permute-done.11 = bf16[1536,512]{1,0:T(8,128)(2,1)} collective-permute-done((bf16[1536,512]{1,0:T(8,128)(2,1)}, bf16[1536,512]{1,0:T(8,128)(2,1)}, u32[]{:S(2)}, u32[]{:S(2)}) %collective-permute-start.11) | collective-permute-done | bytes 1572896 | tf_op jit(solution)/shard_map/ppermute | solution.py:48
  324.3 11.2 %collective-permute-start.12 = (bf16[1536,512]{1,0:T(8,128)(2,1)}, bf16[1536,512]{1,0:T(8,128)(2,1)}, u32[]{:S(2)}, u32[]{:S(2)}) collective-permute-start(bf16[1536,512]{1,0:T(8,128)(2,1)} %collective-permute-done.11), channel_id=1, source_target_pairs={{1,0},{2,1},{5,4},{6,5},{9,8},{10,9},{13,12},{14,13},{17,16},{18,1... | collective-permute-start | bytes 4718600 | tf_op jit(solution)/shard_map/ppermute | solution.py:48
  335.5 22.3 %collective-permute-done.17 = bf16[384,2048]{1,0:T(8,128)(2,1)S(1)} collective-permute-done((bf16[384,2048]{1,0:T(8,128)(2,1)}, bf16[384,2048]{1,0:T(8,128)(2,1)S(1)}, u32[]{:S(2)}, u32[]{:S(2)}) %collective-permute-start.17) | collective-permute-done | bytes 1572896 | tf_op jit(solution)/shard_map/ppermute | solution.py:48
  366.3 6.3 %convolution_convert_fusion.2 = bf16[1536,512]{1,0:T(8,128)(2,1)S(1)} fusion(bf16[1536,2048]{1,0:T(8,128)(2,1)} %select_dynamic-update-slice_fusion.3, bf16[512,2048]{1,0:T(8,128)(2,1)S(1)} %copy-done.11), kind=kOutput, calls=%fused_computation.23 | convolution fusion | flops 3222011904 | bytes 9961472 | tf_op jit(solution)/shard_map/dot_general | solution.py:213
  377.4 11.5 %fusion.3 = bf16[4,4,384,384]{2,3,1,0:T(8,128)(2,1)} fusion(f32[4,384,384,4]{2,1,3,0:T(8,128)S(1)} %fusion.32, f32[4,4,384,384]{2,3,1,0:T(8,128)} %get-tuple-element.80, f32[4,4,384]{2,1,0:T(4,128)S(1)} %copy-done.23), kind=kOutput, calls=%fused_computation.5 | output fusion | flops 14162303 | bytes 23617536 | tf_op jit(solution)/shard_map/sub | solution.py:92
  388.9 5.6 %fusion.41 = bf16[4,384,128]{2,1,0:T(8,128)(2,1)S(1)} fusion(bf16[4,384,4,128]{3,2,1,0:T(4,128)(2,1)} %reshape.151, f32[4,4,384,384]{2,3,1,0:T(8,128)} %get-tuple-element.80, f32[4,4,384]{2,1,0:T(4,128)S(1)} %copy-done.23), kind=kOutput, calls=%fused_computation.61 | convolution fusion | flops 608894976 | bytes 11427840 | tf_op jit(solution)/shard_map/sgqk,sqgd->skd/dot_general | solution.py:100
  405.3 5.5 %convolution_convert_fusion = bf16[2048,768]{1,0:T(8,128)(2,1)S(1)} fusion(bf16[1536,2048]{1,0:T(8,128)(2,1)S(1)} %bitcast.171, bf16[1536,128]{1,0:T(8,128)(2,1)S(1)} %bitcast.177, bf16[1536,128]{1,0:T(8,128)(2,1)S(1)} %bitcast.176, bf16[1536,512]{1,0:T(8,128)(2,1)S(1)} %bitcast.175), kind=kOutput, calls=%fused_computation.15 | convolution fusion | flops 4840488960 | bytes 11796480 | tf_op jit(solution)/shard_map/dot_general | solution.py:229
  418.8 57.4 %collective-permute-done.22 = bf16[1536,512]{1,0:T(8,128)(2,1)S(1)} collective-permute-done((bf16[1536,512]{1,0:T(8,128)(2,1)}, bf16[1536,512]{1,0:T(8,128)(2,1)S(1)}, u32[]{:S(2)}, u32[]{:S(2)}) %collective-permute-start.22) | collective-permute-done | bytes 1572896 | tf_op jit(solution)/shard_map/ppermute | solution.py:48
  484.0 6.3 %add_convert_fusion.1 = bf16[1536,512]{1,0:T(8,128)(2,1)S(1)} fusion(bf16[1536,2048]{1,0:T(8,128)(2,1)} %select_dynamic-update-slice_fusion, bf16[1,2048,512]{2,1,0:T(8,128)(2,1)S(1)} %copy-done.2, bf16[1536,2048]{1,0:T(8,128)(2,1)S(1)} %bitcast.171, s32[]{:T(128)S(6)} %select_n.156), kind=kOutput, calls=%fused_computation.19 | convolution fusion | flops 3223584768 | bytes 11534340 | tf_op jit(solution)/shard_map/dot_general | solution.py:248
  499.6 8.0 %fusion.9 = bf16[1,2048,512]{2,1,0:T(8,128)(2,1)} fusion(bf16[1536,2048]{1,0:T(8,128)(2,1)} %select_dynamic-update-slice_fusion, bf16[1536,2048]{1,0:T(8,128)(2,1)} %select_dynamic-update-slice_fusion.3, s32[]{:T(128)S(6)} %select_n.156), kind=kOutput, calls=%fused_computation.24 | convolution fusion | flops 3222274048 | bytes 9961476 | tf_op jit(solution)/shard_map/dot_general | solution.py:265
  507.6 4.3 fusion.19
  (179 shorter events, 139.1 us)
Async XLA Ops:
  7.2 285.2 %reduce-scatter.2.cloned.1.call-start = ((), (), s32[]{:S(2)}) async-start(), calls=%async_computation.1 | async-start | bytes 4718592 | tf_op jit(solution)/shard_map/reduce_scatter | solution.py:142
  51.5 56.4 %collective-permute-start.3 = (bf16[384,2048]{1,0:T(8,128)(2,1)}, bf16[384,2048]{1,0:T(8,128)(2,1)}, u32[]{:S(2)}, u32[]{:S(2)}) collective-permute-start(bf16[384,2048]{1,0:T(8,128)(2,1)} %collective-permute-done.2), channel_id=1, source_target_pairs={{1,0},{2,1},{5,4},{6,5},{9,8},{10,9},{13,12},{14,13},{17,16},{18,1... | collective-permute-start | bytes 4718600 | tf_op jit(solution)/shard_map/ppermute | solution.py:48
  56.2 61.5 %collective-permute-start.6 = (bf16[512,768]{1,0:T(8,128)(2,1)}, bf16[512,768]{1,0:T(8,128)(2,1)}, u32[]{:S(2)}, u32[]{:S(2)}) collective-permute-start(bf16[512,768]{1,0:T(8,128)(2,1)} %pad_maximum_fusion.2), channel_id=1, source_target_pairs={{0,1},{1,2},{2,3},{3,0},{4,5},{5,6},{6,7},{7,4},{8,9},{9,10},{10,1... | collective-permute-start | bytes 2359304 | tf_op jit(solution)/shard_map/ppermute | solution.py:121
  59.8 83.2 %collective-permute-start.7 = (bf16[512,768]{1,0:T(8,128)(2,1)}, bf16[512,768]{1,0:T(8,128)(2,1)}, u32[]{:S(2)}, u32[]{:S(2)}) collective-permute-start(bf16[512,768]{1,0:T(8,128)(2,1)} %pad_maximum_fusion.3), channel_id=1, source_target_pairs={{0,2},{1,3},{2,0},{3,1},{4,6},{5,7},{6,4},{7,5},{8,10},{9,11},{10,... | collective-permute-start | bytes 2359304 | tf_op jit(solution)/shard_map/ppermute | solution.py:121
  63.2 81.0 %collective-permute-start.8 = (bf16[512,768]{1,0:T(8,128)(2,1)}, bf16[512,768]{1,0:T(8,128)(2,1)}, u32[]{:S(2)}, u32[]{:S(2)}) collective-permute-start(bf16[512,768]{1,0:T(8,128)(2,1)} %pad_maximum_fusion.4), channel_id=1, source_target_pairs={{0,3},{1,0},{2,1},{3,2},{4,7},{5,4},{6,5},{7,6},{8,11},{9,8},{10,9... | collective-permute-start | bytes 2359304 | tf_op jit(solution)/shard_map/ppermute | solution.py:121
  107.9 66.6 %collective-permute-start.4 = (bf16[384,2048]{1,0:T(8,128)(2,1)}, bf16[384,2048]{1,0:T(8,128)(2,1)}, u32[]{:S(2)}, u32[]{:S(2)}) collective-permute-start(bf16[384,2048]{1,0:T(8,128)(2,1)} %collective-permute-done.3), channel_id=1, source_target_pairs={{1,0},{5,4},{9,8},{13,12},{17,16},{21,20},{25,24},{29,28}} | collective-permute-start | bytes 4718600 | tf_op jit(solution)/shard_map/ppermute | solution.py:48
  111.8 395.8 %all-gather.2.cloned.1.call-start = ((), (), s32[]{:S(2)}) async-start(), calls=%async_computation.2 | async-start | bytes 4718592 | tf_op jit(solution)/shard_map/all_gather | solution.py:149
  116.8 61.9 %collective-permute-start.5 = (bf16[384,2048]{1,0:T(8,128)(2,1)}, bf16[384,2048]{1,0:T(8,128)(2,1)S(1)}, u32[]{:S(2)}, u32[]{:S(2)}) collective-permute-start(bf16[384,2048]{1,0:T(8,128)(2,1)} %collective-permute-done.1), channel_id=1, source_target_pairs={{2,3},{6,7},{10,11},{14,15},{18,19},{22,23},{26,27},{30,31}} | collective-permute-start | bytes 4718600 | tf_op jit(solution)/shard_map/ppermute | solution.py:47
  145.4 57.7 %collective-permute-start.13 = (bf16[384,2048]{1,0:T(8,128)(2,1)}, bf16[384,2048]{1,0:T(8,128)(2,1)}, u32[]{:S(2)}, u32[]{:S(2)}) collective-permute-start(bf16[384,2048]{1,0:T(8,128)(2,1)} %param.10), channel_id=1, source_target_pairs={{0,1},{1,2},{2,3},{4,5},{5,6},{6,7},{8,9},{9,10},{10,11},{12,13},{... | collective-permute-start | bytes 4718600 | tf_op jit(solution)/shard_map/ppermute | solution.py:47
  162.3 60.4 %collective-permute-start.15 = (bf16[384,2048]{1,0:T(8,128)(2,1)}, bf16[384,2048]{1,0:T(8,128)(2,1)}, u32[]{:S(2)}, u32[]{:S(2)}) collective-permute-start(bf16[384,2048]{1,0:T(8,128)(2,1)} %param.10), channel_id=1, source_target_pairs={{1,0},{2,1},{3,2},{5,4},{6,5},{7,6},{9,8},{10,9},{11,10},{13,12},{... | collective-permute-start | bytes 4718600 | tf_op jit(solution)/shard_map/ppermute | solution.py:48
  164.8 111.6 %collective-permute-start.19 = (bf16[512,512]{1,0:T(8,128)(2,1)}, bf16[512,512]{1,0:T(8,128)(2,1)}, u32[]{:S(2)}, u32[]{:S(2)}) collective-permute-start(bf16[512,512]{1,0:T(8,128)(2,1)} %get-tuple-element.49), channel_id=1, source_target_pairs={{0,1},{1,2},{2,3},{3,0},{4,5},{5,6},{6,7},{7,4},{8,9},{9,10},{10,1... | collective-permute-start | bytes 1572872 | tf_op jit(solution)/shard_map/ppermute | solution.py:121
  174.4 108.5 %collective-permute-start.20 = (bf16[512,512]{1,0:T(8,128)(2,1)}, bf16[512,512]{1,0:T(8,128)(2,1)}, u32[]{:S(2)}, u32[]{:S(2)}) collective-permute-start(bf16[512,512]{1,0:T(8,128)(2,1)} %get-tuple-element.48), channel_id=1, source_target_pairs={{0,2},{1,3},{2,0},{3,1},{4,6},{5,7},{6,4},{7,5},{8,10},{9,11},{10,... | collective-permute-start | bytes 1572872 | tf_op jit(solution)/shard_map/ppermute | solution.py:121
  178.6 105.8 %collective-permute-start.21 = (bf16[512,512]{1,0:T(8,128)(2,1)}, bf16[512,512]{1,0:T(8,128)(2,1)}, u32[]{:S(2)}, u32[]{:S(2)}) collective-permute-start(bf16[512,512]{1,0:T(8,128)(2,1)} %get-tuple-element.47), channel_id=1, source_target_pairs={{0,3},{1,0},{2,1},{3,2},{4,7},{5,4},{6,5},{7,6},{8,11},{9,8},{10,9... | collective-permute-start | bytes 1572872 | tf_op jit(solution)/shard_map/ppermute | solution.py:121
  222.7 52.4 %collective-permute-start.16 = (bf16[384,2048]{1,0:T(8,128)(2,1)}, bf16[384,2048]{1,0:T(8,128)(2,1)}, u32[]{:S(2)}, u32[]{:S(2)}) collective-permute-start(bf16[384,2048]{1,0:T(8,128)(2,1)} %collective-permute-done.15), channel_id=1, source_target_pairs={{1,0},{2,1},{5,4},{6,5},{9,8},{10,9},{13,12},{14,13},{17,16},{18,1... | collective-permute-start | bytes 4718600 | tf_op jit(solution)/shard_map/ppermute | solution.py:48
  247.3 52.2 %collective-permute-start.9 = (bf16[1536,512]{1,0:T(8,128)(2,1)}, bf16[1536,512]{1,0:T(8,128)(2,1)}, u32[]{:S(2)}, u32[]{:S(2)}) collective-permute-start(bf16[1536,512]{1,0:T(8,128)(2,1)} %bitcast.166), channel_id=1, source_target_pairs={{0,1},{1,2},{2,3},{4,5},{5,6},{6,7},{8,9},{9,10},{10,11},{12,13},{... | collective-permute-start | bytes 4718600 | tf_op jit(solution)/shard_map/ppermute | solution.py:47
  276.4 81.5 %collective-permute-start.17 = (bf16[384,2048]{1,0:T(8,128)(2,1)}, bf16[384,2048]{1,0:T(8,128)(2,1)S(1)}, u32[]{:S(2)}, u32[]{:S(2)}) collective-permute-start(bf16[384,2048]{1,0:T(8,128)(2,1)} %collective-permute-done.16), channel_id=1, source_target_pairs={{1,0},{5,4},{9,8},{13,12},{17,16},{21,20},{25,24},{29,28}} | collective-permute-start | bytes 4718600 | tf_op jit(solution)/shard_map/ppermute | solution.py:48
  285.6 77.4 %collective-permute-start.18 = (bf16[384,2048]{1,0:T(8,128)(2,1)}, bf16[384,2048]{1,0:T(8,128)(2,1)}, u32[]{:S(2)}, u32[]{:S(2)}) collective-permute-start(bf16[384,2048]{1,0:T(8,128)(2,1)} %collective-permute-done.14), channel_id=1, source_target_pairs={{2,3},{6,7},{10,11},{14,15},{18,19},{22,23},{26,27},{30,31}} | collective-permute-start | bytes 4718600 | tf_op jit(solution)/shard_map/ppermute | solution.py:47
  299.5 95.1 %collective-permute-start.10 = (bf16[1536,512]{1,0:T(8,128)(2,1)}, bf16[1536,512]{1,0:T(8,128)(2,1)}, u32[]{:S(2)}, u32[]{:S(2)}) collective-permute-start(bf16[1536,512]{1,0:T(8,128)(2,1)} %collective-permute-done.9), channel_id=1, source_target_pairs={{1,2},{2,3},{5,6},{6,7},{9,10},{10,11},{13,14},{14,15},{17,18},{18... | collective-permute-start | bytes 4718600 | tf_op jit(solution)/shard_map/ppermute | solution.py:47
  324.3 70.3 %collective-permute-start.12 = (bf16[1536,512]{1,0:T(8,128)(2,1)}, bf16[1536,512]{1,0:T(8,128)(2,1)}, u32[]{:S(2)}, u32[]{:S(2)}) collective-permute-start(bf16[1536,512]{1,0:T(8,128)(2,1)} %collective-permute-done.11), channel_id=1, source_target_pairs={{1,0},{2,1},{5,4},{6,5},{9,8},{10,9},{13,12},{14,13},{17,16},{18,1... | collective-permute-start | bytes 4718600 | tf_op jit(solution)/shard_map/ppermute | solution.py:48
  398.8 77.4 %collective-permute-start.22 = (bf16[1536,512]{1,0:T(8,128)(2,1)}, bf16[1536,512]{1,0:T(8,128)(2,1)S(1)}, u32[]{:S(2)}, u32[]{:S(2)}) collective-permute-start(bf16[1536,512]{1,0:T(8,128)(2,1)} %collective-permute-done.12), channel_id=1, source_target_pairs={{1,0},{5,4},{9,8},{13,12},{17,16},{21,20},{25,24},{29,28}} | collective-permute-start | bytes 4718600 | tf_op jit(solution)/shard_map/ppermute | solution.py:48
  400.1 80.7 %collective-permute-start.23 = (bf16[1536,512]{1,0:T(8,128)(2,1)}, bf16[1536,512]{1,0:T(8,128)(2,1)S(1)}, u32[]{:S(2)}, u32[]{:S(2)}) collective-permute-start(bf16[1536,512]{1,0:T(8,128)(2,1)} %collective-permute-done.10), channel_id=1, source_target_pairs={{2,3},{6,7},{10,11},{14,15},{18,19},{22,23},{26,27},{30,31}} | collective-permute-start | bytes 4718600 | tf_op jit(solution)/shard_map/ppermute | solution.py:47
  411.0 83.0 %collective-permute-start.27 = (bf16[512,768]{1,0:T(8,128)(2,1)S(1)}, bf16[512,768]{1,0:T(8,128)(2,1)S(1)}, u32[]{:S(2)}, u32[]{:S(2)}) collective-permute-start(bf16[512,768]{1,0:T(8,128)(2,1)S(1)} %get-tuple-element.44), channel_id=1, source_target_pairs={{0,1},{1,2},{2,3},{3,0},{4,5},{5,6},{6,7},{7,4},{8,9},{9,10},{10,1... | collective-permute-start | bytes 2359304 | tf_op jit(solution)/shard_map/ppermute | solution.py:121
  413.8 83.0 %collective-permute-start.28 = (bf16[512,768]{1,0:T(8,128)(2,1)S(1)}, bf16[512,768]{1,0:T(8,128)(2,1)S(1)}, u32[]{:S(2)}, u32[]{:S(2)}) collective-permute-start(bf16[512,768]{1,0:T(8,128)(2,1)S(1)} %get-tuple-element.43), channel_id=1, source_target_pairs={{0,2},{1,3},{2,0},{3,1},{4,6},{5,7},{6,4},{7,5},{8,10},{9,11},{10,... | collective-permute-start | bytes 2359304 | tf_op jit(solution)/shard_map/ppermute | solution.py:121
  413.8 83.0 %collective-permute-start.29 = (bf16[512,768]{1,0:T(8,128)(2,1)S(1)}, bf16[512,768]{1,0:T(8,128)(2,1)S(1)}, u32[]{:S(2)}, u32[]{:S(2)}) collective-permute-start(bf16[512,768]{1,0:T(8,128)(2,1)S(1)} %get-tuple-element.42), channel_id=1, source_target_pairs={{0,3},{1,0},{2,1},{3,2},{4,7},{5,4},{6,5},{7,6},{8,11},{9,8},{10,9... | collective-permute-start | bytes 2359304 | tf_op jit(solution)/shard_map/ppermute | solution.py:121
  (34 other events, 507.3 us)
Sparse Core Ops, SparseCore 0:
  111.9 68.8 reduce-scatter.1
  295.0 52.4 all-gather.1

commit v4 on v3

--- a/solution.py
+++ b/solution.py
@@ -181,9 +181,10 @@
         jnp.zeros((total_rows, width), jnp.bfloat16),
         (cotangent, w_output),
     )
-    all_cotangent, _ = gather(
-        later_cotangent, place_rows, jnp.zeros((total_rows, width), jnp.bfloat16)
-    )
+    cotangent_blocks, _ = relay(later_cotangent)
+    all_cotangent = jnp.zeros((total_rows, width), jnp.bfloat16)
+    for j in range(n):
+        all_cotangent = place_rows(all_cotangent, cotangent_blocks[j], lax.rem(me + n - j, n))
 
     def pick_weight(d):
         return jnp.concatenate(
@@ -209,16 +210,16 @@
     attn, saved = attend(query_raw, key_raw, value_raw)
 
     own_attn = attn.reshape(total_rows, own_query)
-    d_attn = (
-        lax.dot_general(
-            all_cotangent,
+    d_attn = jnp.zeros((total_rows, own_query), jnp.bfloat16)
+    for j in (0, 1, 3, 2) if n == 4 else range(n):
+        part = lax.dot_general(
+            cotangent_blocks[j],
             w_out_rows,
             (((1,), (1,)), ((), ())),
             preferred_element_type=jnp.float32,
-        )
-        .astype(jnp.bfloat16)
-        .reshape(n, length, group, HEAD_SIZE)
-    )
+        ).astype(jnp.bfloat16)
+        d_attn = place_rows(d_attn, part, lax.rem(me + n - j, n))
+    d_attn = d_attn.reshape(n, length, group, HEAD_SIZE)
     all_attn, d_scores = gather(
         own_attn,
         place_cols,

time: 530 us -> 532 us (level)
  starting transfers between devices: 112 us -> 120 us
  waiting for transfers between devices: 233 us -> 226 us
    ppermute x9, waiting for transfers between devices: 172 us -> 160 us  [relay(): lax.ppermute(last_down, 'fsdp', [(f, f - 1) for f in range(1, n - hop + 1)])]
    ppermute x9, starting transfers between devices: 21.8 us -> 12.2 us  [relay(): lax.ppermute(last_down, 'fsdp', [(f, f - 1) for f in range(1, n - hop + 1)])]
    ppermute x12, starting transfers between devices: 30.2 us -> 38.8 us  [send(): lax.ppermute(pick(lax.rem(me + shift, n)), 'fsdp', [(f, (f + shift) % n)...]
    ppermute x9, starting transfers between devices: 60.2 us -> 68.5 us  [relay(): lax.ppermute(last_up, 'fsdp', [(f, f + 1) for f in range(hop - 1, n - 1)])]
  transfers between devices with their start and end apart: 32 -> 32, of which waited for: 10 -> 11; matrix products, arithmetic and copies ran while one was open for 30% -> 30% of each run, Pallas kernels for 0% -> 0%
where the time goes in v4:
time: 532 us; the launch traced here: 526 us
  waiting for transfers between devices  226 us (42%)
  starting transfers between devices  120 us (23%)
  matrix products  62.2 us (12%)
  other arithmetic  52.7 us (10%)
  local copies, waits for them, and re-layouts  49.8 us (9%)
  between operations  15.4 us (3%)
    ppermute x9, waiting for transfers between devices, relay(): lax.ppermute(last_down, 'fsdp', [(f, f - 1) for f in range(1, n - hop + 1)])  160 us
    ppermute x9, starting transfers between devices, relay(): lax.ppermute(last_up, 'fsdp', [(f, f + 1) for f in range(hop - 1, n - 1)])  68.5 us
    ppermute x12, starting transfers between devices, send(): lax.ppermute(pick(lax.rem(me + shift, n)), 'fsdp', [(f, (f + shift) % n)...  38.8 us
    ppermute x9, waiting for transfers between devices, relay(): lax.ppermute(last_up, 'fsdp', [(f, f + 1) for f in range(hop - 1, n - 1)])  38 us
    ppermute x12, waiting for transfers between devices, send(): lax.ppermute(pick(lax.rem(me + shift, n)), 'fsdp', [(f, (f + shift) % n)...  28.6 us
    dynamic_update_slice x17, local copies, waits for them, and re-layouts, place_cols(): return lax.dynamic_update_slice_in_dim(out, piece, f * piece.shape[1], 1)  12.6 us
    dynamic_update_slice x7, other arithmetic, place_rows(): return lax.dynamic_update_slice_in_dim(out, piece, f * piece.shape[0], 0)  12.6 us
    ppermute x9, starting transfers between devices, relay(): lax.ppermute(last_down, 'fsdp', [(f, f - 1) for f in range(1, n - hop + 1)])  12.2 us
  transfers between devices with their start and end apart: 32, of which 11 were waited for; matrix products, arithmetic and copies ran while one was open for 30% of the time, Pallas kernels for 0%

profile of v4, /device:TPU:0, one launch (start us, length us, event | category | flops | bytes accessed | tf_op | source)
XLA Modules:
  0.0 525.8 jit_solution(17778094043729969503)
XLA Ops:
  7.2 6.2 %collective-permute-start = (bf16[384,2048]{1,0:T(8,128)(2,1)}, bf16[384,2048]{1,0:T(8,128)(2,1)}, u32[]{:S(2)}, u32[]{:S(2)}) collective-permute-start(bf16[384,2048]{1,0:T(8,128)(2,1)} %param.9), channel_id=1, source_target_pairs={{0,1},{1,2},{2,3},{4,5},{5,6},{6,7},{8,9},{9,10},{10,11},{12,13},{... | collective-permute-start | bytes 4718600 | tf_op jit(solution)/shard_map/ppermute | solution.py:47
  14.8 31.5 %collective-permute-done = bf16[384,2048]{1,0:T(8,128)(2,1)} collective-permute-done((bf16[384,2048]{1,0:T(8,128)(2,1)}, bf16[384,2048]{1,0:T(8,128)(2,1)}, u32[]{:S(2)}, u32[]{:S(2)}) %collective-permute-start) | collective-permute-done | bytes 1572896 | tf_op jit(solution)/shard_map/ppermute | solution.py:47
  48.0 3.5 collective-permute-done.2
  69.8 38.1 %collective-permute-done.3 = bf16[384,2048]{1,0:T(8,128)(2,1)} collective-permute-done((bf16[384,2048]{1,0:T(8,128)(2,1)}, bf16[384,2048]{1,0:T(8,128)(2,1)}, u32[]{:S(2)}, u32[]{:S(2)}) %collective-permute-start.3) | collective-permute-done | bytes 1572896 | tf_op jit(solution)/shard_map/ppermute | solution.py:48
  114.4 28.6 %collective-permute-done.7 = bf16[512,768]{1,0:T(8,128)(2,1)} collective-permute-done((bf16[512,768]{1,0:T(8,128)(2,1)}, bf16[512,768]{1,0:T(8,128)(2,1)}, u32[]{:S(2)}, u32[]{:S(2)}) %collective-permute-start.7) | collective-permute-done | bytes 786464 | tf_op jit(solution)/shard_map/ppermute | solution.py:121
  146.1 16.1 %collective-permute-start.16 = (bf16[384,2048]{1,0:T(8,128)(2,1)}, bf16[384,2048]{1,0:T(8,128)(2,1)}, u32[]{:S(2)}, u32[]{:S(2)}) collective-permute-start(bf16[384,2048]{1,0:T(8,128)(2,1)} %param.10), channel_id=1, source_target_pairs={{0,1},{1,2},{2,3},{4,5},{5,6},{6,7},{8,9},{9,10},{10,11},{12,13},{... | collective-permute-start | bytes 4718600 | tf_op jit(solution)/shard_map/ppermute | solution.py:47
  169.7 4.6 collective-permute-done.4
  178.6 17.8 %collective-permute-start.15 = (bf16[512,512]{1,0:T(8,128)(2,1)}, bf16[512,512]{1,0:T(8,128)(2,1)}, u32[]{:S(2)}, u32[]{:S(2)}) collective-permute-start(bf16[512,512]{1,0:T(8,128)(2,1)} %get-tuple-element.47), channel_id=1, source_target_pairs={{0,3},{1,0},{2,1},{3,2},{4,7},{5,4},{6,5},{7,6},{8,11},{9,8},{10,9... | collective-permute-start | bytes 1572872 | tf_op jit(solution)/shard_map/ppermute | solution.py:121
  198.5 5.2 fusion.64
  212.5 9.6 %collective-permute-done.18 = bf16[384,2048]{1,0:T(8,128)(2,1)} collective-permute-done((bf16[384,2048]{1,0:T(8,128)(2,1)}, bf16[384,2048]{1,0:T(8,128)(2,1)}, u32[]{:S(2)}, u32[]{:S(2)}) %collective-permute-start.18) | collective-permute-done | bytes 1572896 | tf_op jit(solution)/shard_map/ppermute | solution.py:48
  229.6 10.1 %fusion.63 = (f32[4,4,384]{2,1,0:T(4,128)}, f32[4,4,384,384]{2,3,1,0:T(8,128)}) fusion(pred[384,384]{0,1:T(8,128)(4,1)} %iota_compare_fusion, bf16[4,384,1,64]{3,1,0,2:T(8,128)(2,1)} %get-tuple-element.61, bf16[4,384,1,64]{3,1,0,2:T(8,128)(2,1)} %get-tuple-element.60, bf16[4,384,4,64]{3,1,2,0:T(8,128)(2,1)S(1)} %get-tuple-element.39, ...), kind=kOutput, calls=%fused_computation.148 | convolution fusion | flops 617349504 | bytes 11575296 | tf_op jit(solution)/shard_map/sub | solution.py:82
  239.7 4.8 fusion.28
  247.2 37.1 %collective-permute-start.9 = (bf16[1536,512]{1,0:T(8,128)(2,1)}, bf16[1536,512]{1,0:T(8,128)(2,1)}, u32[]{:S(2)}, u32[]{:S(2)}) collective-permute-start(bf16[1536,512]{1,0:T(8,128)(2,1)} %bitcast.169), channel_id=1, source_target_pairs={{0,1},{1,2},{2,3},{4,5},{5,6},{6,7},{8,9},{9,10},{10,11},{12,13},{... | collective-permute-start | bytes 4718600 | tf_op jit(solution)/shard_map/ppermute | solution.py:47
  304.0 6.5 %collective-permute-done.9 = bf16[1536,512]{1,0:T(8,128)(2,1)} collective-permute-done((bf16[1536,512]{1,0:T(8,128)(2,1)}, bf16[1536,512]{1,0:T(8,128)(2,1)}, u32[]{:S(2)}, u32[]{:S(2)}) %collective-permute-start.9) | collective-permute-done | bytes 1572896 | tf_op jit(solution)/shard_map/ppermute | solution.py:47
  312.3 20.2 %collective-permute-done.11 = bf16[1536,512]{1,0:T(8,128)(2,1)} collective-permute-done((bf16[1536,512]{1,0:T(8,128)(2,1)}, bf16[1536,512]{1,0:T(8,128)(2,1)}, u32[]{:S(2)}, u32[]{:S(2)}) %collective-permute-start.11) | collective-permute-done | bytes 1572896 | tf_op jit(solution)/shard_map/ppermute | solution.py:48
  333.9 32.2 %collective-permute-done.20 = bf16[384,2048]{1,0:T(8,128)(2,1)} collective-permute-done((bf16[384,2048]{1,0:T(8,128)(2,1)}, bf16[384,2048]{1,0:T(8,128)(2,1)}, u32[]{:S(2)}, u32[]{:S(2)}) %collective-permute-start.20) | collective-permute-done | bytes 1572896 | tf_op jit(solution)/shard_map/ppermute | solution.py:48
  379.0 11.6 %fusion.3 = bf16[4,4,384,384]{2,3,1,0:T(8,128)(2,1)} fusion(f32[4,384,384,4]{2,1,3,0:T(8,128)S(1)} %fusion.32, f32[4,4,384,384]{2,3,1,0:T(8,128)} %get-tuple-element.80, f32[4,4,384]{2,1,0:T(4,128)S(1)} %copy-done.23), kind=kOutput, calls=%fused_computation.5 | output fusion | flops 14162303 | bytes 23617536 | tf_op jit(solution)/shard_map/sub | solution.py:92
  390.6 5.6 %fusion.41 = bf16[4,384,128]{2,1,0:T(8,128)(2,1)S(1)} fusion(bf16[4,384,4,128]{3,2,1,0:T(4,128)(2,1)} %reshape.151, f32[4,4,384,384]{2,3,1,0:T(8,128)} %get-tuple-element.80, f32[4,4,384]{2,1,0:T(4,128)S(1)} %copy-done.23), kind=kOutput, calls=%fused_computation.60 | convolution fusion | flops 608894976 | bytes 11427840 | tf_op jit(solution)/shard_map/sgqk,sqgd->skd/dot_general | solution.py:100
  407.0 5.5 %convolution_convert_fusion = bf16[2048,768]{1,0:T(8,128)(2,1)S(1)} fusion(bf16[1536,2048]{1,0:T(8,128)(2,1)S(1)} %bitcast.174, bf16[1536,128]{1,0:T(8,128)(2,1)S(1)} %bitcast.182, bf16[1536,128]{1,0:T(8,128)(2,1)S(1)} %bitcast.181, bf16[1536,512]{1,0:T(8,128)(2,1)S(1)} %bitcast.180), kind=kOutput, calls=%fused_computation.15 | convolution fusion | flops 4840488960 | bytes 11796480 | tf_op jit(solution)/shard_map/dot_general | solution.py:230
  427.1 50.8 %collective-permute-done.22 = bf16[1536,512]{1,0:T(8,128)(2,1)S(1)} collective-permute-done((bf16[1536,512]{1,0:T(8,128)(2,1)}, bf16[1536,512]{1,0:T(8,128)(2,1)S(1)}, u32[]{:S(2)}, u32[]{:S(2)}) %collective-permute-start.22) | collective-permute-done | bytes 1572896 | tf_op jit(solution)/shard_map/ppermute | solution.py:48
  485.8 6.3 %add_convert_fusion.1 = bf16[1536,512]{1,0:T(8,128)(2,1)S(1)} fusion(bf16[1536,2048]{1,0:T(8,128)(2,1)} %select_dynamic-update-slice_fusion, bf16[1,2048,512]{2,1,0:T(8,128)(2,1)S(1)} %copy-done.2, bf16[1536,2048]{1,0:T(8,128)(2,1)S(1)} %bitcast.174, s32[]{:T(128)S(6)} %select_n.160), kind=kOutput, calls=%fused_computation.19 | convolution fusion | flops 3223584768 | bytes 11534340 | tf_op jit(solution)/shard_map/dot_general | solution.py:249
  495.5 4.0 collective-permute-start.26
  502.3 7.6 %fusion.9 = bf16[1,2048,512]{2,1,0:T(8,128)(2,1)} fusion(bf16[1536,2048]{1,0:T(8,128)(2,1)} %select_dynamic-update-slice_fusion, bf16[1536,2048]{1,0:T(8,128)(2,1)S(1)} %fusion.54, s32[]{:T(128)S(6)} %select_n.160), kind=kOutput, calls=%fused_computation.23 | convolution fusion | flops 3222274048 | bytes 9961476 | tf_op jit(solution)/shard_map/dot_general | solution.py:266
  509.9 4.3 fusion.19
  (188 shorter events, 142.4 us)
Async XLA Ops:
  7.2 294.3 %reduce-scatter.2.cloned.1.call-start = ((), (), s32[]{:S(2)}) async-start(), calls=%async_computation.1 | async-start | bytes 4718592 | tf_op jit(solution)/shard_map/reduce_scatter | solution.py:142
  51.5 56.4 %collective-permute-start.3 = (bf16[384,2048]{1,0:T(8,128)(2,1)}, bf16[384,2048]{1,0:T(8,128)(2,1)}, u32[]{:S(2)}, u32[]{:S(2)}) collective-permute-start(bf16[384,2048]{1,0:T(8,128)(2,1)} %collective-permute-done.2), channel_id=1, source_target_pairs={{1,0},{2,1},{5,4},{6,5},{9,8},{10,9},{13,12},{14,13},{17,16},{18,1... | collective-permute-start | bytes 4718600 | tf_op jit(solution)/shard_map/ppermute | solution.py:48
  56.3 56.7 %collective-permute-start.6 = (bf16[512,768]{1,0:T(8,128)(2,1)}, bf16[512,768]{1,0:T(8,128)(2,1)}, u32[]{:S(2)}, u32[]{:S(2)}) collective-permute-start(bf16[512,768]{1,0:T(8,128)(2,1)} %pad_maximum_fusion.2), channel_id=1, source_target_pairs={{0,1},{1,2},{2,3},{3,0},{4,5},{5,6},{6,7},{7,4},{8,9},{9,10},{10,1... | collective-permute-start | bytes 2359304 | tf_op jit(solution)/shard_map/ppermute | solution.py:121
  59.8 83.1 %collective-permute-start.7 = (bf16[512,768]{1,0:T(8,128)(2,1)}, bf16[512,768]{1,0:T(8,128)(2,1)}, u32[]{:S(2)}, u32[]{:S(2)}) collective-permute-start(bf16[512,768]{1,0:T(8,128)(2,1)} %pad_maximum_fusion.3), channel_id=1, source_target_pairs={{0,2},{1,3},{2,0},{3,1},{4,6},{5,7},{6,4},{7,5},{8,10},{9,11},{10,... | collective-permute-start | bytes 2359304 | tf_op jit(solution)/shard_map/ppermute | solution.py:121
  63.2 81.7 %collective-permute-start.8 = (bf16[512,768]{1,0:T(8,128)(2,1)}, bf16[512,768]{1,0:T(8,128)(2,1)}, u32[]{:S(2)}, u32[]{:S(2)}) collective-permute-start(bf16[512,768]{1,0:T(8,128)(2,1)} %pad_maximum_fusion.4), channel_id=1, source_target_pairs={{0,3},{1,0},{2,1},{3,2},{4,7},{5,4},{6,5},{7,6},{8,11},{9,8},{10,9... | collective-permute-start | bytes 2359304 | tf_op jit(solution)/shard_map/ppermute | solution.py:121
  68.6 441.3 %all-gather.2.cloned.1.call-start = ((), (), s32[]{:S(2)}) async-start(), calls=%async_computation.2 | async-start | bytes 4718592 | tf_op jit(solution)/shard_map/all_gather | solution.py:149
  107.9 66.5 %collective-permute-start.4 = (bf16[384,2048]{1,0:T(8,128)(2,1)}, bf16[384,2048]{1,0:T(8,128)(2,1)}, u32[]{:S(2)}, u32[]{:S(2)}) collective-permute-start(bf16[384,2048]{1,0:T(8,128)(2,1)} %collective-permute-done.3), channel_id=1, source_target_pairs={{1,0},{5,4},{9,8},{13,12},{17,16},{21,20},{25,24},{29,28}} | collective-permute-start | bytes 4718600 | tf_op jit(solution)/shard_map/ppermute | solution.py:48
  146.1 64.6 %collective-permute-start.16 = (bf16[384,2048]{1,0:T(8,128)(2,1)}, bf16[384,2048]{1,0:T(8,128)(2,1)}, u32[]{:S(2)}, u32[]{:S(2)}) collective-permute-start(bf16[384,2048]{1,0:T(8,128)(2,1)} %param.10), channel_id=1, source_target_pairs={{0,1},{1,2},{2,3},{4,5},{5,6},{6,7},{8,9},{9,10},{10,11},{12,13},{... | collective-permute-start | bytes 4718600 | tf_op jit(solution)/shard_map/ppermute | solution.py:47
  162.2 60.0 %collective-permute-start.18 = (bf16[384,2048]{1,0:T(8,128)(2,1)}, bf16[384,2048]{1,0:T(8,128)(2,1)}, u32[]{:S(2)}, u32[]{:S(2)}) collective-permute-start(bf16[384,2048]{1,0:T(8,128)(2,1)} %param.10), channel_id=1, source_target_pairs={{1,0},{2,1},{3,2},{5,4},{6,5},{7,6},{9,8},{10,9},{11,10},{13,12},{... | collective-permute-start | bytes 4718600 | tf_op jit(solution)/shard_map/ppermute | solution.py:48
  164.7 121.3 %collective-permute-start.13 = (bf16[512,512]{1,0:T(8,128)(2,1)}, bf16[512,512]{1,0:T(8,128)(2,1)}, u32[]{:S(2)}, u32[]{:S(2)}) collective-permute-start(bf16[512,512]{1,0:T(8,128)(2,1)} %get-tuple-element.49), channel_id=1, source_target_pairs={{0,1},{1,2},{2,3},{3,0},{4,5},{5,6},{6,7},{7,4},{8,9},{9,10},{10,1... | collective-permute-start | bytes 1572872 | tf_op jit(solution)/shard_map/ppermute | solution.py:121
  174.4 115.4 %collective-permute-start.14 = (bf16[512,512]{1,0:T(8,128)(2,1)}, bf16[512,512]{1,0:T(8,128)(2,1)}, u32[]{:S(2)}, u32[]{:S(2)}) collective-permute-start(bf16[512,512]{1,0:T(8,128)(2,1)} %get-tuple-element.48), channel_id=1, source_target_pairs={{0,2},{1,3},{2,0},{3,1},{4,6},{5,7},{6,4},{7,5},{8,10},{9,11},{10,... | collective-permute-start | bytes 1572872 | tf_op jit(solution)/shard_map/ppermute | solution.py:121
  178.6 112.4 %collective-permute-start.15 = (bf16[512,512]{1,0:T(8,128)(2,1)}, bf16[512,512]{1,0:T(8,128)(2,1)}, u32[]{:S(2)}, u32[]{:S(2)}) collective-permute-start(bf16[512,512]{1,0:T(8,128)(2,1)} %get-tuple-element.47), channel_id=1, source_target_pairs={{0,3},{1,0},{2,1},{3,2},{4,7},{5,4},{6,5},{7,6},{8,11},{9,8},{10,9... | collective-permute-start | bytes 1572872 | tf_op jit(solution)/shard_map/ppermute | solution.py:121
  222.2 62.6 %collective-permute-start.19 = (bf16[384,2048]{1,0:T(8,128)(2,1)}, bf16[384,2048]{1,0:T(8,128)(2,1)}, u32[]{:S(2)}, u32[]{:S(2)}) collective-permute-start(bf16[384,2048]{1,0:T(8,128)(2,1)} %collective-permute-done.18), channel_id=1, source_target_pairs={{1,0},{2,1},{5,4},{6,5},{9,8},{10,9},{13,12},{14,13},{17,16},{18,1... | collective-permute-start | bytes 4718600 | tf_op jit(solution)/shard_map/ppermute | solution.py:48
  247.2 63.2 %collective-permute-start.9 = (bf16[1536,512]{1,0:T(8,128)(2,1)}, bf16[1536,512]{1,0:T(8,128)(2,1)}, u32[]{:S(2)}, u32[]{:S(2)}) collective-permute-start(bf16[1536,512]{1,0:T(8,128)(2,1)} %bitcast.169), channel_id=1, source_target_pairs={{0,1},{1,2},{2,3},{4,5},{5,6},{6,7},{8,9},{9,10},{10,11},{12,13},{... | collective-permute-start | bytes 4718600 | tf_op jit(solution)/shard_map/ppermute | solution.py:47
  284.7 47.7 %collective-permute-start.11 = (bf16[1536,512]{1,0:T(8,128)(2,1)}, bf16[1536,512]{1,0:T(8,128)(2,1)}, u32[]{:S(2)}, u32[]{:S(2)}) collective-permute-start(bf16[1536,512]{1,0:T(8,128)(2,1)} %bitcast.169), channel_id=1, source_target_pairs={{1,0},{2,1},{3,2},{5,4},{6,5},{7,6},{9,8},{10,9},{11,10},{13,12},{... | collective-permute-start | bytes 4718600 | tf_op jit(solution)/shard_map/ppermute | solution.py:48
  286.0 80.1 %collective-permute-start.20 = (bf16[384,2048]{1,0:T(8,128)(2,1)}, bf16[384,2048]{1,0:T(8,128)(2,1)}, u32[]{:S(2)}, u32[]{:S(2)}) collective-permute-start(bf16[384,2048]{1,0:T(8,128)(2,1)} %collective-permute-done.19), channel_id=1, source_target_pairs={{1,0},{5,4},{9,8},{13,12},{17,16},{21,20},{25,24},{29,28}} | collective-permute-start | bytes 4718600 | tf_op jit(solution)/shard_map/ppermute | solution.py:48
  292.1 77.2 %collective-permute-start.21 = (bf16[384,2048]{1,0:T(8,128)(2,1)}, bf16[384,2048]{1,0:T(8,128)(2,1)}, u32[]{:S(2)}, u32[]{:S(2)}) collective-permute-start(bf16[384,2048]{1,0:T(8,128)(2,1)} %collective-permute-done.17), channel_id=1, source_target_pairs={{2,3},{6,7},{10,11},{14,15},{18,19},{22,23},{26,27},{30,31}} | collective-permute-start | bytes 4718600 | tf_op jit(solution)/shard_map/ppermute | solution.py:47
  310.4 85.9 %collective-permute-start.10 = (bf16[1536,512]{1,0:T(8,128)(2,1)}, bf16[1536,512]{1,0:T(8,128)(2,1)}, u32[]{:S(2)}, u32[]{:S(2)}) collective-permute-start(bf16[1536,512]{1,0:T(8,128)(2,1)} %collective-permute-done.9), channel_id=1, source_target_pairs={{1,2},{2,3},{5,6},{6,7},{9,10},{10,11},{13,14},{14,15},{17,18},{18... | collective-permute-start | bytes 4718600 | tf_op jit(solution)/shard_map/ppermute | solution.py:47
  332.5 63.8 %collective-permute-start.12 = (bf16[1536,512]{1,0:T(8,128)(2,1)}, bf16[1536,512]{1,0:T(8,128)(2,1)}, u32[]{:S(2)}, u32[]{:S(2)}) collective-permute-start(bf16[1536,512]{1,0:T(8,128)(2,1)} %collective-permute-done.11), channel_id=1, source_target_pairs={{1,0},{2,1},{5,4},{6,5},{9,8},{10,9},{13,12},{14,13},{17,16},{18,1... | collective-permute-start | bytes 4718600 | tf_op jit(solution)/shard_map/ppermute | solution.py:48
  400.5 77.4 %collective-permute-start.22 = (bf16[1536,512]{1,0:T(8,128)(2,1)}, bf16[1536,512]{1,0:T(8,128)(2,1)S(1)}, u32[]{:S(2)}, u32[]{:S(2)}) collective-permute-start(bf16[1536,512]{1,0:T(8,128)(2,1)} %collective-permute-done.12), channel_id=1, source_target_pairs={{1,0},{5,4},{9,8},{13,12},{17,16},{21,20},{25,24},{29,28}} | collective-permute-start | bytes 4718600 | tf_op jit(solution)/shard_map/ppermute | solution.py:48
  401.8 80.8 %collective-permute-start.23 = (bf16[1536,512]{1,0:T(8,128)(2,1)}, bf16[1536,512]{1,0:T(8,128)(2,1)S(1)}, u32[]{:S(2)}, u32[]{:S(2)}) collective-permute-start(bf16[1536,512]{1,0:T(8,128)(2,1)} %collective-permute-done.10), channel_id=1, source_target_pairs={{2,3},{6,7},{10,11},{14,15},{18,19},{22,23},{26,27},{30,31}} | collective-permute-start | bytes 4718600 | tf_op jit(solution)/shard_map/ppermute | solution.py:47
  412.7 82.8 %collective-permute-start.27 = (bf16[512,768]{1,0:T(8,128)(2,1)S(1)}, bf16[512,768]{1,0:T(8,128)(2,1)S(1)}, u32[]{:S(2)}, u32[]{:S(2)}) collective-permute-start(bf16[512,768]{1,0:T(8,128)(2,1)S(1)} %get-tuple-element.44), channel_id=1, source_target_pairs={{0,1},{1,2},{2,3},{3,0},{4,5},{5,6},{6,7},{7,4},{8,9},{9,10},{10,1... | collective-permute-start | bytes 2359304 | tf_op jit(solution)/shard_map/ppermute | solution.py:121
  415.5 84.0 %collective-permute-start.28 = (bf16[512,768]{1,0:T(8,128)(2,1)S(1)}, bf16[512,768]{1,0:T(8,128)(2,1)S(1)}, u32[]{:S(2)}, u32[]{:S(2)}) collective-permute-start(bf16[512,768]{1,0:T(8,128)(2,1)S(1)} %get-tuple-element.43), channel_id=1, source_target_pairs={{0,2},{1,3},{2,0},{3,1},{4,6},{5,7},{6,4},{7,5},{8,10},{9,11},{10,... | collective-permute-start | bytes 2359304 | tf_op jit(solution)/shard_map/ppermute | solution.py:121
  415.5 84.0 %collective-permute-start.29 = (bf16[512,768]{1,0:T(8,128)(2,1)S(1)}, bf16[512,768]{1,0:T(8,128)(2,1)S(1)}, u32[]{:S(2)}, u32[]{:S(2)}) collective-permute-start(bf16[512,768]{1,0:T(8,128)(2,1)S(1)} %get-tuple-element.42), channel_id=1, source_target_pairs={{0,3},{1,0},{2,1},{3,2},{4,7},{5,4},{6,5},{7,6},{8,11},{9,8},{10,9... | collective-permute-start | bytes 2359304 | tf_op jit(solution)/shard_map/ppermute | solution.py:121
  (36 other events, 556.6 us)
Sparse Core Ops, SparseCore 0:
  68.8 49.5 reduce-scatter.1
  304.1 52.0 all-gather.1
